TPU v7x, 512 devices: a whole 4x4x16 slice. The times are simulated.
512 devices in a mesh: prow: 32 (over z, y_lo), pcol: 16 (over y_hi, x, core).
Axes of the slice: x: 4, y: 4 (y_hi: 2, y_lo: 2; y = y_hi * 2 + y_lo), z: 16, core: 2. Of those that a mesh axis runs over, the one named last changes fastest.
Arguments:
- orb_valence: bfloat16 [16384, 1000], P(('prow', 'pcol')), may hold values from -1.75 to 1.75
- orb_conduction: bfloat16 [16384, 1000], P(('prow', 'pcol')), may hold values from -1.75 to 1.75
- screened: bfloat16 [16384, 16384], P('prow', 'pcol'), may hold values from -0.046875 to 0.046875
- bare: bfloat16 [16384, 16384], P('prow', 'pcol'), may hold values from -0.046875 to 0.046875
- panel_valence: int32 [128], replicated, may hold values from 0 to 999
- panel_conduction: int32 [128], replicated, may hold values from 0 to 999
Outputs:
- kernel_panel: float32 [12000, 128], P('prow', 'pcol')
All inputs are finite; a program needn't handle non-finite values.
Results may differ from a plain program's by a relative error of at most 0.004.
Values may be sent and summed in bfloat16 or wider, within the bound.
A program may use at most 64 MiB of HBM per device.

v0:
```python
import jax
import jax.numpy as jnp
from jax import lax
from jax.sharding import PartitionSpec as P

NCW = 12


def broadcast(value, axis, source):
    kept = jnp.where(lax.axis_index(axis) == source, value, 0).astype(value.dtype)
    return lax.psum(kept, axis)


def pair_terms(valence_pick, conduction_pick, conduction_low):
    tile_rows = valence_pick.shape[0]
    panel_width = valence_pick.shape[1]
    band_window = conduction_low.shape[1]
    pair_direct = (
        (
            conduction_pick.astype(jnp.float32)[:, :, None]
            * conduction_low.astype(jnp.float32)[:, None, :]
        )
        .astype(jnp.bfloat16)
        .reshape(tile_rows, panel_width * band_window)
    )
    pair_exchange = (valence_pick.astype(jnp.float32) * conduction_pick.astype(jnp.float32)).astype(
        jnp.bfloat16
    )
    return (pair_direct, pair_exchange)


def body(orb_valence, orb_conduction, screened, bare, panel_valence, panel_conduction):
    col_count = lax.axis_size("pcol")
    row_count = lax.axis_size("prow")
    group_ratio = row_count // col_count
    col_index = lax.axis_index("pcol")
    band_window = NCW
    panel_width = panel_valence.shape[0]
    per_column = panel_width // col_count
    valence_block, conduction_block = (
        lax.all_gather(orb_valence, "pcol", axis=0, tiled=True),
        lax.all_gather(orb_conduction, "pcol", axis=0, tiled=True),
    )
    conduction_low = conduction_block[:, :band_window]
    conduction_pick = jnp.take(conduction_block, panel_conduction, axis=1)
    valence_pick = jnp.take(valence_block, panel_valence, axis=1)
    tile_rows = valence_block.shape[0]
    direct_cols = panel_width * band_window
    direct_acc = jnp.zeros((tile_rows, direct_cols), jnp.float32)
    exchange_acc = jnp.zeros((tile_rows, panel_width), jnp.float32)
    pair_direct, pair_exchange = pair_terms(valence_pick, conduction_pick, conduction_low)
    packed = jnp.concatenate([pair_direct, pair_exchange], axis=1)
    for section in range(group_ratio):
        received = broadcast(packed, "prow", group_ratio * col_index + section)
        screen_part = screened[:, section * tile_rows : (section + 1) * tile_rows]
        bare_part = bare[:, section * tile_rows : (section + 1) * tile_rows]
        direct_acc = direct_acc + jnp.dot(
            screen_part, received[:, :direct_cols], preferred_element_type=jnp.float32
        )
        exchange_acc = exchange_acc + jnp.dot(
            bare_part, received[:, direct_cols:], preferred_element_type=jnp.float32
        )
    direct_sum, exchange_sum = (
        lax.psum_scatter(direct_acc, "pcol", scatter_dimension=1, tiled=True),
        lax.psum_scatter(exchange_acc, "pcol", scatter_dimension=1, tiled=True),
    )
    valence_own = lax.dynamic_slice_in_dim(valence_pick, col_index * per_column, per_column, 1)
    combined = 2.0 * conduction_low.astype(jnp.float32)[:, None, :] * exchange_sum[
        :, :, None
    ] - valence_own.astype(jnp.float32)[:, :, None] * direct_sum.reshape(
        tile_rows, per_column, band_window
    )
    combined = combined.astype(jnp.bfloat16)
    summand = jnp.einsum("mv,mjc->cvj", valence_block, combined, preferred_element_type=jnp.float32)
    summand = summand.reshape(band_window * valence_block.shape[1], per_column)
    return lax.psum_scatter(summand, "prow", scatter_dimension=0, tiled=True)


def solution(mesh):
    placed = (
        P(("prow", "pcol"), None),
        P(("prow", "pcol"), None),
        P("prow", "pcol"),
        P("prow", "pcol"),
        P(),
        P(),
    )
    return jax.shard_map(
        body, mesh=mesh, in_specs=placed, out_specs=P("prow", "pcol"), check_vma=False
    )
```

profile of v0, /device:TPU:6, one launch (start us, length us, event | category | flops | bytes accessed | tf_op | source)
XLA Modules:
  0.0 811.9 jit_solution(6417512345122995570)
XLA Ops:
  6.5 0.0 copy-start.4
  6.5 0.0 all-reduce.7.cloned.1.call-start
  6.5 0.7 compare_select_fusion
  7.2 0.7 compare_select_fusion.1
  7.9 0.7 compare_and_fusion
  8.6 23.7 %all_gather.7 = bf16[512,1000]{1,0:T(8,128)(2,1)S(1)} all-gather(bf16[32,1000]{1,0:T(8,128)(2,1)} %param.8), channel_id=1, replica_groups=mesh['prow'=32,'pcol'=16] {'pcol'}, dimensions={0}, use_global_device_ids=true | all-gather | bytes 1088000 | tf_op jit(solution)/shard_map/all_gather | solution.py:41
  32.3 1.4 copy.20
  33.7 0.0 copy-done.4
  33.7 22.5 %all_gather.6 = bf16[512,1000]{1,0:T(8,128)(2,1)S(1)} all-gather(bf16[32,1000]{1,0:T(8,128)(2,1)S(1)} %copy-done.4), channel_id=1, replica_groups=mesh['prow'=32,'pcol'=16] {'pcol'}, dimensions={0}, use_global_device_ids=true | all-gather | bytes 1088000 | tf_op jit(solution)/shard_map/all_gather | solution.py:42
  56.2 0.5 copy.18
  56.7 0.0 copy-start.1
  56.7 0.8 gather_fusion
  57.6 0.2 copy-done.1
  57.7 0.1 bitcast_convert_fusion
  57.8 0.7 multiply_convert_fusion
  58.5 1.3 convert_element_type.33
  59.9 0.0 copy-start
  59.9 2.3 gather_fusion.1
  62.2 0.1 multiply_convert_fusion.1
  62.3 0.0 copy-done
  62.4 2.3 broadcast_select_fusion
  64.7 0.0 all-reduce.7.cloned.1.call-update
  64.7 0.0 reduce-scatter.6.cloned.1.call-start
  64.7 283.8 %all-reduce.7.cloned.1.call-done = (bf16[512,1664]{0,1:T(8,128)(2,1)}, bf16[512,1664]{0,1:T(8,128)(2,1)}) async-done(((bf16[512,1664]{0,1:T(8,128)(2,1)}, bf16[512,1664]{0,1:T(8,128)(2,1)}), (bf16[512,1664]{0,1:T(8,128)(2,1)}, bf16[512,1664]{0,1:T(8,128)(2,1)})) %all-reduce.7.cloned.1.call-update) | async-done | bytes 3407888 | tf_op jit(solution)/shard_map/psum | solution.py:11
  348.6 0.0 copy-start.2
  348.6 0.0 copy-start.3
  348.6 2.7 fusion.2
  351.2 0.0 copy-done.2
  351.2 0.0 copy-done.3
  351.3 2.7 fusion
  353.9 0.0 reduce-scatter.6.cloned.1.call-update
  354.0 0.0 reduce-scatter.4.cloned.1.call-start
  354.0 1.4 fusion.9
  355.4 2.1 fusion.4
  357.5 0.0 reduce-scatter.4.cloned.1.call-update
  357.5 0.0 all-reduce.5.cloned.1.call-start
  357.6 0.7 broadcast_multiply_fusion
  358.3 90.7 %reduce-scatter.6.cloned.1.call-done = f32[512,96]{0,1:T(8,128)} async-done(((f32[512,1536]{0,1:T(8,128)}), f32[512,96]{0,1:T(8,128)}) %reduce-scatter.6.cloned.1.call-update) | async-done | bytes 196624 | tf_op jit(solution)/shard_map/reduce_scatter | solution.py:64
  449.0 0.9 reshape.22
  450.0 91.3 %reduce-scatter.4.cloned.1.call-done = f32[512,8]{0,1:T(8,128)} async-done(((f32[512,128]{0,1:T(8,128)}), f32[512,8]{0,1:T(8,128)}) %reduce-scatter.4.cloned.1.call-update) | async-done | bytes 16400 | tf_op jit(solution)/shard_map/reduce_scatter | solution.py:65
  541.3 1.0 convolution_bitcast_fusion
  542.3 1.0 reshape.23
  543.3 0.0 all-reduce.5.cloned.1.call-update
  543.3 1.3 dynamic-slice
  545.3 258.7 %all-reduce.5.cloned.1.call-done = f32[12000,8]{0,1:T(8,128)} async-done(((f32[12000,8]{0,1:T(8,128)}), f32[12000,8]{0,1:T(8,128)}) %all-reduce.5.cloned.1.call-update) | async-done | bytes 384016
  803.9 1.4 constant_dynamic-slice_fusion
  (4 shorter events, 0.0 us)
Async XLA Ops:
  6.5 27.2 %copy-start.4 = (bf16[32,1000]{1,0:T(8,128)(2,1)S(1)}, bf16[32,1000]{1,0:T(8,128)(2,1)}, u32[]{:S(2)}) copy-start(bf16[32,1000]{1,0:T(8,128)(2,1)} %param.9) | copy-start | bytes 192004
  6.5 342.0 %all-reduce.7.cloned.1.call-start = ((), (), s32[]{:S(2)}) async-start(), calls=%async_computation.5 | async-start | bytes 6815744 | tf_op jit(solution)/shard_map/psum | solution.py:11
  56.7 1.0 copy-start.1
  59.9 2.5 copy-start
  64.7 384.3 %reduce-scatter.6.cloned.1.call-start = ((), (), s32[]{:S(2)}) async-start(), calls=%async_computation.3 | async-start | bytes 3342336 | tf_op jit(solution)/shard_map/reduce_scatter | solution.py:64
  348.6 2.7 copy-start.2
  348.6 2.7 copy-start.3
  354.0 187.3 %reduce-scatter.4.cloned.1.call-start = ((), (), s32[]{:S(2)}) async-start(), calls=%async_computation.2 | async-start | bytes 278528 | tf_op jit(solution)/shard_map/reduce_scatter | solution.py:65
  357.5 446.4 %all-reduce.5.cloned.1.call-start = ((), (), s32[]{:S(2)}) async-start(), calls=%async_computation.4 | async-start | bytes 770048
Sparse Core Ops, SparseCore 0:
  64.8 283.7 all-reduce.6
  354.2 94.7 reduce-scatter.5
  454.3 86.9 reduce-scatter.3
  544.0 259.8 all-reduce.4
where the time goes:
time: 812 us
  waiting for transfers between devices  725 us (89%)
  blocking collectives  46.2 us (6%)
  between operations  13.9 us (2%)
  local copies, waits for them, and re-layouts  11.2 us (1%)
  matrix products  9.84 us (1%)
    psum x1, waiting for transfers between devices, broadcast(): return lax.psum(kept, axis)  284 us
    unnamed x5, waiting for transfers between devices  259 us
    reduce_scatter x1, waiting for transfers between devices, body(): lax.psum_scatter(exchange_acc, 'pcol', scatter_dimension=1, tiled=True)  91.3 us
    reduce_scatter x1, waiting for transfers between devices, body(): lax.psum_scatter(direct_acc, 'pcol', scatter_dimension=1, tiled=True)  90.7 us
    all_gather x1, blocking collectives, body(): lax.all_gather(orb_valence, 'pcol', axis=0, tiled=True)  23.7 us
    all_gather x1, blocking collectives, body(): lax.all_gather(orb_conduction, 'pcol', axis=0, tiled=True)  22.5 us
  transfers between devices with their start and end apart: 4, of which 4 were waited for; matrix products, arithmetic and copies ran while one was open for 1% of the time, Pallas kernels for 0%

commit v1 on v0

v1 whole, which is shorter than its diff:
```python
import jax
import jax.numpy as jnp
from jax import lax
from jax.experimental import pallas as pl
from jax.experimental.pallas import tpu as pltpu
from jax.sharding import PartitionSpec as P

NCW = 12
NZ = 16
NCOL = 16
PTS = 32
ROWS = PTS * NCOL
COLS = 1024
NB = 1000
NBP = 1024
HALF = 6
SEG = 375
SEGP = 384
BF = jnp.bfloat16
F32 = jnp.float32
MESH = pl.DeviceIdType.MESH
NT = (((1,), (1,)), ((), ()))


def iota(shape, dim):
    return lax.broadcasted_iota(jnp.int32, shape, dim)


def onehot(mask):
    return jnp.where(mask, 1.0, 0.0).astype(BF)


def kernel(
    v_ref, c_ref, pv_ref, pc_ref, pvs_ref, w_ref, b_ref, out_ref,
    blk, cpad, g_all, got, picks, lows, low_f32, turned, left, left_e,
    w_all, b_all, send0, send1, recv0, recv1, panel, seg_out, seg_in, total, y_in,
    loc_sem, wb_ssem, wb_rsem, a_ssem, a_rsem, g_ssem, g_rsem, h_ssem, h_rsem,
    f_ssem, f_rsem, b_ssem, b_rsem, c_ssem, c_rsem, y_ssem, y_rsem,
):
    row = lax.axis_index("prow")
    col = lax.axis_index("pcol")
    z = lax.div(row, 2)
    ylo = lax.rem(row, 2)
    core = lax.rem(col, 2)
    chip = lax.div(col, 2)
    mate = col + 1 - 2 * core
    other_row = row + 1 - 2 * ylo

    def remote(src, dst, ssem, rsem, prow, pcol):
        return pltpu.make_async_remote_copy(
            src_ref=src, dst_ref=dst, send_sem=ssem, recv_sem=rsem,
            device_id={"prow": prow, "pcol": pcol}, device_id_type=MESH,
        )

    w_local = pltpu.make_async_copy(w_ref, w_all.at[core], loc_sem.at[0])
    b_local = pltpu.make_async_copy(b_ref, b_all.at[core], loc_sem.at[1])
    w_local.start()
    b_local.start()

    barrier = pltpu.get_barrier_semaphore()

    def greet(prow, pcol):
        pl.semaphore_signal(barrier, inc=1, device_id={"prow": prow, "pcol": pcol}, device_id_type=MESH)

    def greet_step(i, _):
        @pl.when((i != z) | (col != z))
        def _():
            greet(2 * i + ylo, z)

        @pl.when((i != col) | (col != z))
        def _():
            greet(2 * col + ylo, i)

        @pl.when(i != col)
        def _():
            greet(row, i)

        @pl.when(i != z)
        def _():
            greet(2 * i + ylo, col)

        return 0

    lax.fori_loop(0, NZ, greet_step, 0)
    greet(other_row, col)
    greet(other_row, mate)

    val = v_ref[...]
    con = c_ref[...]
    bands = iota((NB, 128), 0)
    lanes = iota((NB, 128), 1)
    vp = jnp.dot(val, onehot(bands == pv_ref[...]), preferred_element_type=F32)
    cp = jnp.dot(con, onehot(bands == pc_ref[...]), preferred_element_type=F32)
    lane = iota((PTS, 128), 1)
    blk[0:PTS, :] = jnp.where(lane < 64, cp, pltpu.roll(vp, 64, 1)).astype(BF)
    blk[PTS : 2 * PTS, :] = jnp.where(lane < 64, pltpu.roll(cp, 64, 1), vp).astype(BF)
    cpad[...] = jnp.zeros((128, NB), BF)
    cpad[pl.ds(pl.multiple_of(lax.rem(col, 4) * PTS, PTS), PTS), :] = con
    low_rows = iota((16, NB), 0)
    low_sel = onehot((low_rows == iota((16, NB), 1)) & (low_rows < NCW))
    blk[2 * PTS :, :] = lax.dot_general(low_sel, cpad[...], NT, preferred_element_type=F32).astype(BF)
    tail = jnp.dot(val, onehot((bands == lanes + 896) & (lanes < 104)), preferred_element_type=F32)
    tail = tail + jnp.dot(con, onehot((bands + 104 == lanes) & (bands < NCW)), preferred_element_type=F32)
    g_all[pl.ds(col, 1), :, 0:896] = val[:, 0:896].reshape(1, PTS, 896)
    g_all[pl.ds(col, 1), :, 896:NBP] = tail.astype(BF).reshape(1, PTS, 128)

    w_local.wait()
    b_local.wait()
    same = jnp.where(col == z, 2, 0)
    pl.semaphore_wait(barrier, 64 - same)

    def a_copy(i):
        return remote(blk, got.at[col], a_ssem.at[i], a_rsem.at[col], 2 * i + ylo, z)

    def a_start(i, _):
        there = lax.rem(z + 8 + i, NZ)

        @pl.when((there != z) | (col != z))
        def _():
            a_copy(there).start()

        return 0

    lax.fori_loop(0, NZ, a_start, 0)

    @pl.when(col == z)
    def _():
        got[pl.ds(col, 1)] = blk[...].reshape(1, 80, 128)

    w_copy = remote(w_ref, w_all.at[core], wb_ssem.at[0], wb_rsem.at[0], row, mate)
    b_copy = remote(b_ref, b_all.at[core], wb_ssem.at[1], wb_rsem.at[1], row, mate)
    w_copy.start()
    b_copy.start()

    def g_copy(k):
        return remote(g_all.at[col], g_all.at[col], g_ssem.at[k], g_rsem.at[chip], row, 2 * k + core)

    def g_start(i, _):
        there = lax.rem(chip + i, 8)
        g_copy(there).start()
        return 0

    lax.fori_loop(1, 8, g_start, 0)

    def h_copy(k, mine):
        slot = 2 * k + mine
        return remote(g_all.at[slot], g_all.at[slot], h_ssem.at[k], h_rsem.at[k], row, mate)

    h_copy(chip, core).start()

    def a_recv(i, _):
        @pl.when((i != col) | (col != z))
        def _():
            remote(blk, got.at[i], a_ssem.at[i], a_rsem.at[i], row, mate).wait_recv()

        return 0

    lax.fori_loop(0, NCOL, a_recv, 0)

    def pick_own(i, _):
        picks[core, ylo, pl.ds(i, 1)] = got[pl.ds(i, 1), pl.ds(pl.multiple_of(core * PTS, PTS), PTS), :]
        return 0

    lax.fori_loop(0, NCOL, pick_own, 0)
    for g in range(4):
        part = got[4 * g, 64:80, :].astype(F32)
        for s in range(1, 4):
            part = part + got[4 * g + s, 64:80, :].astype(F32)
        lows[core, ylo, :, g * 128 : (g + 1) * 128] = part.astype(BF)

    there_half = got.at[:, pl.ds(pl.multiple_of((1 - core) * PTS, PTS), PTS), :]
    own_half = picks.at[core, ylo]
    own_low = lows.at[core, ylo]
    slot = core * 2 + ylo
    passes = []
    for n, (src, prow, pcol) in enumerate(
        ((there_half, row, mate), (own_half, other_row, col), (there_half, other_row, mate))
    ):
        passes.append(remote(src, picks.at[core, ylo], f_ssem.at[0, n], f_rsem.at[0, slot], prow, pcol))
        passes.append(remote(own_low, lows.at[core, ylo], f_ssem.at[1, n], f_rsem.at[1, slot], prow, pcol))
    for copy in passes:
        copy.start()

    def h_start(i, _):
        k = lax.rem(chip + i, 8)
        remote(g_all.at[col], g_all.at[2 * k + core], g_ssem.at[k], g_rsem.at[k], row, mate).wait_recv()
        h_copy(k, core).start()
        return 0

    lax.fori_loop(1, 8, h_start, 0)

    for n in range(4):
        @pl.when(slot != n)
        def _(n=n):
            a, b = n // 2, n % 2
            remote(own_half, picks.at[a, b], f_ssem.at[0, 0], f_rsem.at[0, n], row, mate).wait_recv()
            remote(own_low, lows.at[a, b], f_ssem.at[1, 0], f_rsem.at[1, n], row, mate).wait_recv()

    eye = onehot(iota((128, 128), 0) == iota((128, 128), 1))
    for n in range(4):
        a, b = n // 2, n % 2
        turned[:, n * ROWS : (n + 1) * ROWS] = lax.dot_general(
            eye, picks[a, b].reshape(ROWS, 128), NT, preferred_element_type=F32
        )
        low_f32[:, n * ROWS : (n + 1) * ROWS] = lows[a, b].astype(F32)

    w_copy.wait_recv()
    b_copy.wait_recv()
    left_e[...] = (turned[0:64, :] * turned[64:128, :]).astype(BF)

    def against(lhs, rhs, n):
        rows = pl.ds(pl.multiple_of(n * 256, 256), 256)
        return lax.dot_general(lhs[:, 0:COLS], rhs[0, rows, :], NT, preferred_element_type=F32) + lax.dot_general(
            lhs[:, COLS:], rhs[1, rows, :], NT, preferred_element_type=F32
        )

    far = 1 - lax.div(z, 8)

    def build(half):
        def step(m, _):
            tile = turned[pl.ds(pl.multiple_of(m * 8, 8), 8), :]
            for p in range(HALF // 2):
                first = half * HALF + 2 * p
                pair = jnp.concatenate(
                    [tile * low_f32[pl.ds(first, 1), :], tile * low_f32[pl.ds(first + 1, 1), :]], axis=0
                )
                left[pl.ds(pl.multiple_of(m * 48 + 16 * p, 16), 16), :] = pair.astype(BF)
            return 0

        lax.fori_loop(0, 8, step, 0)

    def b_copy_to(n, m):
        sends, recvs = ((send0, recv0), (send1, recv1))[n]
        return remote(sends.at[m], recvs.at[chip], b_ssem.at[n, m], b_rsem.at[n, chip], row, 8 * core + m)

    order = (far, 1 - far)
    for n in range(2):
        sends, recvs = ((send0, recv0), (send1, recv1))[n]
        build(order[n])

        def mul(t, _, n=n, sends=sends):
            span = pl.ds(pl.multiple_of(t * 256, 256), 256)
            d = against(left[...], w_all, t).astype(BF)
            for m in range(8):
                sends[m, 0:48, span] = d[m * 48 : (m + 1) * 48, :]
            if n == 0:
                e = against(left_e[...], b_all, t)
                head = e.astype(BF).astype(F32)
                rest = e - head
                for m in range(8):
                    both = jnp.concatenate([head[m * 8 : m * 8 + 8], rest[m * 8 : m * 8 + 8]], axis=0)
                    sends[m, 48:64, span] = both.astype(BF)
            return 0

        lax.fori_loop(0, 2, mul, 0)

        def b_start(m, _, n=n, sends=sends, recvs=recvs):
            @pl.when(8 * core + m != col)
            def _():
                b_copy_to(n, m).start()

            @pl.when(8 * core + m == col)
            def _():
                recvs[pl.ds(chip, 1)] = sends[pl.ds(m, 1)]

            return 0

        lax.fori_loop(0, 8, b_start, 0)

    def h_wait(i, _):
        h_copy(i, 1 - core).wait_recv()
        return 0

    lax.fori_loop(0, 8, h_wait, 0)
    points = g_all[...].reshape(ROWS, NBP)
    mine = jnp.zeros((8, NBP), jnp.int32)
    for i in range(8):
        mine = jnp.where(iota((8, NBP), 0) == i, pvs_ref[col * 8 + i], mine)
    sel = onehot(mine == iota((8, NBP), 1))
    vpt = lax.dot_general(sel, points, NT, preferred_element_type=F32)
    sel = onehot((iota((16, NBP), 1) == iota((16, NBP), 0) + NB) & (iota((16, NBP), 0) < NCW))
    low_f32[:, 0:ROWS] = lax.dot_general(sel, points, NT, preferred_element_type=F32)

    def b_recv(n):
        recvs = (recv0, recv1)[n]

        def step(k, _):
            @pl.when(2 * k + lax.div(col, 8) != col)
            def _():
                remote(recvs.at[k], recvs.at[k], b_ssem.at[n, 0], b_rsem.at[n, k], row, mate).wait_recv()

            return 0

        lax.fori_loop(0, 8, step, 0)

    def c_copy(i):
        return remote(seg_out.at[i], seg_in.at[z], c_ssem.at[i], c_rsem.at[z], 2 * i + ylo, col)

    lane = iota((8, SEGP), 1)
    for n in range(2):
        recvs = (recv0, recv1)[n]
        half = order[n]
        b_recv(n)
        d = recvs[0].astype(F32)
        for k in range(1, 8):
            d = d + recvs[k].astype(F32)
        if n == 0:
            exch = 2.0 * (d[48:56] + d[56:64])
        comb = [
            low_f32[pl.ds(half * HALF + i, 1), 0:ROWS] * exch - vpt * d[i * 8 : i * 8 + 8] for i in range(HALF)
        ]
        comb = jnp.concatenate(comb, axis=0).astype(BF)
        panel[...] = jnp.dot(comb, points, preferred_element_type=F32)
        for zl in range(8):
            halves = []
            for y in range(2):
                start = SEG * (2 * zl + y)
                band0, off = start // NB, start % NB
                seg = panel[band0 * 8 : band0 * 8 + 8, :]
                if off:
                    seg = pltpu.roll(seg, NBP - off, 1)
                seg = seg[:, 0:SEGP]
                if off + SEG > NB:
                    more = pltpu.roll(panel[band0 * 8 + 8 : band0 * 8 + 16, :], NB - off, 1)[:, 0:SEGP]
                    seg = jnp.where(lane < NB - off, seg, more)
                halves.append(seg)
            seg_out[pl.ds(half * 8 + zl, 1)] = jnp.concatenate(halves, axis=0).astype(BF).reshape(1, 16, SEGP)

        def c_start(i, _, half=half):
            there = half * 8 + i

            @pl.when(there != z)
            def _():
                c_copy(there).start()

            @pl.when(there == z)
            def _():
                seg_in[pl.ds(z, 1)] = seg_out[pl.ds(z, 1)]

            return 0

        lax.fori_loop(0, 8, c_start, 0)

    def c_recv(i, _):
        @pl.when(i != z)
        def _():
            remote(seg_out.at[i], seg_in.at[i], c_ssem.at[i], c_rsem.at[i], row, mate).wait_recv()

        return 0

    lax.fori_loop(0, NZ, c_recv, 0)
    acc = seg_in[0].astype(F32)
    for i in range(1, NZ):
        acc = acc + seg_in[i].astype(F32)
    total[...] = acc.reshape(2, 8, SEGP)
    y_copy = remote(total.at[1 - ylo], y_in, y_ssem, y_rsem, other_row, col)
    y_copy.start()

    def drain(i, _):
        @pl.when((i != z) | (col != z))
        def _():
            a_copy(i).wait_send()

        @pl.when(i != z)
        def _():
            c_copy(i).wait_send()

        return 0

    lax.fori_loop(0, NZ, drain, 0)

    def drain8(i, _):
        @pl.when(i != chip)
        def _():
            g_copy(i).wait_send()

        h_copy(i, core).wait_send()

        @pl.when(8 * core + i != col)
        def _():
            b_copy_to(0, i).wait_send()
            b_copy_to(1, i).wait_send()

        return 0

    lax.fori_loop(0, 8, drain8, 0)
    for copy in passes:
        copy.wait_send()
    w_copy.wait_send()
    b_copy.wait_send()
    y_copy.wait()
    out_ref[...] = total[ylo] + y_in[...]


def body(orb_valence, orb_conduction, screened, bare, panel_valence, panel_conduction):
    vmem = pl.BlockSpec(memory_space=pltpu.VMEM)
    hbm = pl.BlockSpec(memory_space=pl.ANY)
    dma = pltpu.SemaphoreType.DMA
    out = pl.pallas_call(
        kernel,
        out_shape=jax.ShapeDtypeStruct((8, SEGP), F32),
        in_specs=[vmem, vmem, vmem, vmem, pl.BlockSpec(memory_space=pltpu.SMEM), hbm, hbm],
        out_specs=vmem,
        scratch_shapes=[
            pltpu.VMEM((80, 128), BF),
            pltpu.VMEM((128, NB), BF),
            pltpu.VMEM((NCOL, PTS, NBP), BF),
            pltpu.VMEM((NCOL, 80, 128), BF),
            pltpu.VMEM((2, 2, NCOL, PTS, 128), BF),
            pltpu.VMEM((2, 2, 16, ROWS), BF),
            pltpu.VMEM((16, 2 * COLS), F32),
            pltpu.VMEM((128, 2 * COLS), F32),
            pltpu.VMEM((8 * HALF * 8, 2 * COLS), BF),
            pltpu.VMEM((64, 2 * COLS), BF),
            pltpu.VMEM((2, ROWS, COLS), BF),
            pltpu.VMEM((2, ROWS, COLS), BF),
            pltpu.VMEM((8, 64, ROWS), BF),
            pltpu.VMEM((8, 48, ROWS), BF),
            pltpu.VMEM((8, 64, ROWS), BF),
            pltpu.VMEM((8, 48, ROWS), BF),
            pltpu.VMEM((48, NBP), F32),
            pltpu.VMEM((NZ, 16, SEGP), BF),
            pltpu.VMEM((NZ, 16, SEGP), BF),
            pltpu.VMEM((2, 8, SEGP), F32),
            pltpu.VMEM((8, SEGP), F32),
            dma((2,)),
            dma((2,)), dma((2,)),
            dma((16,)), dma((16,)),
            dma((8,)), dma((8,)),
            dma((8,)), dma((8,)),
            dma((2, 3)), dma((2, 4)),
            dma((2, 8)), dma((2, 8)),
            dma((16,)), dma((16,)),
            dma, dma,
        ],
        compiler_params=pltpu.CompilerParams(
            collective_id=0, has_side_effects=True, vmem_limit_bytes=48 * 2**20
        ),
        name="kernel_panel",
    )(
        orb_valence, orb_conduction, panel_valence.reshape(1, -1), panel_conduction.reshape(1, -1),
        panel_valence, screened, bare,
    )
    return out[:, :SEG].T


def solution(mesh):
    placed = (
        P(("prow", "pcol"), None),
        P(("prow", "pcol"), None),
        P("prow", "pcol"),
        P("prow", "pcol"),
        P(),
        P(),
    )
    return jax.shard_map(
        body, mesh=mesh, in_specs=placed, out_specs=P("prow", "pcol"), check_vma=False
    )
```

time: 812 us -> 80.5 us (0.10)
  the two profiles are of different devices: /device:TPU:6 before, /device:TPU:1 now
where the time goes in v1:
time: 80.5 us; the launch traced here: 79 us
  Pallas kernels  73.6 us (91%)
  local copies, waits for them, and re-layouts  5.4 us (7%)
    pallas_call x1, Pallas kernels, body(): pl.pallas_call(kernel, out_shape=jax.ShapeDtypeStruct((8, SEGP), F32), in...  73.6 us
    unnamed x12, local copies, waits for them, and re-layouts  4.8 us

profile of v1, /device:TPU:1, one launch (start us, length us, event | category | flops | bytes accessed | tf_op | source)
XLA Modules:
  0.0 79.0 jit_solution(9110259293802428983)
XLA Ops:
  0.0 0.0 copy-start.4
  0.0 0.0 copy-start.5
  0.0 0.7 copy-done.4
  0.7 0.0 copy-done.5
  0.7 0.0 copy-start
  0.7 1.2 %copy-done = bf16[512,1024]{1,0:T(8,128)(2,1)S(1)} copy-done((bf16[512,1024]{1,0:T(8,128)(2,1)S(1)}, bf16[512,1024]{1,0:T(8,128)(2,1)}, u32[]{:S(2)}) %copy-start) | copy-done | bytes 1048600
  1.9 0.0 copy-start.1
  1.9 1.2 %copy-done.1 = bf16[512,1024]{1,0:T(8,128)(2,1)S(1)} copy-done((bf16[512,1024]{1,0:T(8,128)(2,1)S(1)}, bf16[512,1024]{1,0:T(8,128)(2,1)}, u32[]{:S(2)}) %copy-start.1) | copy-done | bytes 1048600
  3.1 0.0 copy-start.2
  3.1 0.8 %copy-done.2 = bf16[32,1000]{1,0:T(8,128)(2,1)S(1)} copy-done((bf16[32,1000]{1,0:T(8,128)(2,1)S(1)}, bf16[32,1000]{1,0:T(8,128)(2,1)}, u32[]{:S(2)}) %copy-start.2) | copy-done | bytes 64024
  4.0 0.0 copy-start.3
  4.0 0.8 %copy-done.3 = bf16[32,1000]{1,0:T(8,128)(2,1)S(1)} copy-done((bf16[32,1000]{1,0:T(8,128)(2,1)S(1)}, bf16[32,1000]{1,0:T(8,128)(2,1)}, u32[]{:S(2)}) %copy-start.3) | copy-done | bytes 64024
  4.8 73.6 %kernel_panel.1 = f32[8,384]{1,0:T(8,128)S(1)} custom-call(bf16[32,1000]{1,0:T(8,128)(2,1)S(1)} %copy-done.2, bf16[32,1000]{1,0:T(8,128)(2,1)S(1)} %copy-done.3, s32[1,128]{1,0:T(1,128)S(1)} %bitcast.4, s32[1,128]{1,0:T(1,128)S(1)} %bitcast.5, s32[128]{0:T(128)S(1)} %copy-done.4, bf16[512,1024]{1,0:T(8,128)(2,1)S(1)} %copy-done, bf16[512,1024]{1,0:T(8,128)(2,1)S(1)} %copy-done.1), custom_call_target="tpu_custom_call" | custom-call | tf_op jit(solution)/shard_map/kernel_panel/pallas_call | solution.py:399
  78.4 0.6 slice_bitcast_fusion
Async XLA Ops:
  0.0 0.7 copy-start.4
  0.0 0.7 copy-start.5
  0.7 1.2 %copy-start = (bf16[512,1024]{1,0:T(8,128)(2,1)S(1)}, bf16[512,1024]{1,0:T(8,128)(2,1)}, u32[]{:S(2)}) copy-start(bf16[512,1024]{1,0:T(8,128)(2,1)} %w_ref.1) | copy-start | bytes 3145732
  1.9 1.2 %copy-start.1 = (bf16[512,1024]{1,0:T(8,128)(2,1)S(1)}, bf16[512,1024]{1,0:T(8,128)(2,1)}, u32[]{:S(2)}) copy-start(bf16[512,1024]{1,0:T(8,128)(2,1)} %b_ref.1) | copy-start | bytes 3145732
  3.1 0.8 %copy-start.2 = (bf16[32,1000]{1,0:T(8,128)(2,1)S(1)}, bf16[32,1000]{1,0:T(8,128)(2,1)}, u32[]{:S(2)}) copy-start(bf16[32,1000]{1,0:T(8,128)(2,1)} %v_ref.1) | copy-start | bytes 192004
  4.0 0.8 %copy-start.3 = (bf16[32,1000]{1,0:T(8,128)(2,1)S(1)}, bf16[32,1000]{1,0:T(8,128)(2,1)}, u32[]{:S(2)}) copy-start(bf16[32,1000]{1,0:T(8,128)(2,1)} %c_ref.1) | copy-start | bytes 192004

commit v2 on v1

--- a/solution.py
+++ b/solution.py
@@ -16,6 +16,8 @@
 HALF = 6
 SEG = 375
 SEGP = 384
+HUBS = (0, 3, -3, 6, -6)
+SECOND = tuple((n, d) for n in range(5) for d in ((-1, 0, 1, 2) if n == 3 else (-1, 0, 1)))
 BF = jnp.bfloat16
 F32 = jnp.float32
 MESH = pl.DeviceIdType.MESH
@@ -31,10 +33,11 @@
 
 
 def kernel(
-    v_ref, c_ref, pv_ref, pc_ref, pvs_ref, w_ref, b_ref, out_ref,
-    blk, cpad, g_all, got, picks, lows, low_f32, turned, left, left_e,
+    v_hbm, c_hbm, pv_hbm, pc_hbm, w_ref, b_ref, out_ref,
+    v_ref, c_ref, pv_ref, pc_ref,
+    hub, cpad, g_all, got, picks, lows, low_f32, turned, left, left_e,
     w_all, b_all, send0, send1, recv0, recv1, panel, seg_out, seg_in, total, y_in,
-    loc_sem, wb_ssem, wb_rsem, a_ssem, a_rsem, g_ssem, g_rsem, h_ssem, h_rsem,
+    loc_sem, wb_ssem, wb_rsem, a_ssem, a_rsem, s_ssem, s_rsem, g_ssem, g_rsem, h_ssem, h_rsem,
     f_ssem, f_rsem, b_ssem, b_rsem, c_ssem, c_rsem, y_ssem, y_rsem,
 ):
     row = lax.axis_index("prow")
@@ -46,30 +49,42 @@
     mate = col + 1 - 2 * core
     other_row = row + 1 - 2 * ylo
 
+    def around(i):
+        return lax.rem(i + NZ, NZ)
+
     def remote(src, dst, ssem, rsem, prow, pcol):
         return pltpu.make_async_remote_copy(
             src_ref=src, dst_ref=dst, send_sem=ssem, recv_sem=rsem,
             device_id={"prow": prow, "pcol": pcol}, device_id_type=MESH,
         )
 
-    w_local = pltpu.make_async_copy(w_ref, w_all.at[core], loc_sem.at[0])
-    b_local = pltpu.make_async_copy(b_ref, b_all.at[core], loc_sem.at[1])
-    w_local.start()
-    b_local.start()
+    loads = [
+        pltpu.make_async_copy(src, dst, loc_sem.at[n])
+        for n, (src, dst) in enumerate(
+            ((c_hbm, c_ref), (pc_hbm, pc_ref), (v_hbm, v_ref), (pv_hbm, pv_ref), (w_ref, w_all.at[0]), (b_ref, b_all.at[0]))
+        )
+    ]
+    for copy in loads:
+        copy.start()
 
     barrier = pltpu.get_barrier_semaphore()
 
     def greet(prow, pcol):
         pl.semaphore_signal(barrier, inc=1, device_id={"prow": prow, "pcol": pcol}, device_id_type=MESH)
 
+    ahead = around(z - col)
+    step = jnp.where(ahead == 8, 2, lax.rem(ahead + 1, 3) - 1)
+    step = jnp.where(ahead > 8, 1 - lax.rem(17 - ahead, 3), step)
+    hub_z = around(z - step)
+
+    def self_step():
+        return hub_z == z
+
     def greet_step(i, _):
-        @pl.when((i != z) | (col != z))
-        def _():
-            greet(2 * i + ylo, z)
-
-        @pl.when((i != col) | (col != z))
-        def _():
-            greet(2 * col + ylo, i)
+        for y in range(2):
+            @pl.when((2 * hub_z + y != row) | (i != col))
+            def _(y=y):
+                greet(2 * hub_z + y, i)
 
         @pl.when(i != col)
         def _():
@@ -82,9 +97,12 @@
         return 0
 
     lax.fori_loop(0, NZ, greet_step, 0)
+    for n in range(1, 5):
+        greet(2 * around(z - HUBS[n]) + ylo, col)
     greet(other_row, col)
-    greet(other_row, mate)
-
+
+    for copy in loads[:4]:
+        copy.wait()
     val = v_ref[...]
     con = c_ref[...]
     bands = iota((NB, 128), 0)
@@ -92,46 +110,55 @@
     vp = jnp.dot(val, onehot(bands == pv_ref[...]), preferred_element_type=F32)
     cp = jnp.dot(con, onehot(bands == pc_ref[...]), preferred_element_type=F32)
     lane = iota((PTS, 128), 1)
-    blk[0:PTS, :] = jnp.where(lane < 64, cp, pltpu.roll(vp, 64, 1)).astype(BF)
-    blk[PTS : 2 * PTS, :] = jnp.where(lane < 64, pltpu.roll(cp, 64, 1), vp).astype(BF)
+    hub[0, 0:PTS, :] = jnp.where(lane < 64, cp, pltpu.roll(vp, 64, 1)).astype(BF)
+    hub[0, PTS : 2 * PTS, :] = jnp.where(lane < 64, pltpu.roll(cp, 64, 1), vp).astype(BF)
     cpad[...] = jnp.zeros((128, NB), BF)
     cpad[pl.ds(pl.multiple_of(lax.rem(col, 4) * PTS, PTS), PTS), :] = con
     low_rows = iota((16, NB), 0)
     low_sel = onehot((low_rows == iota((16, NB), 1)) & (low_rows < NCW))
-    blk[2 * PTS :, :] = lax.dot_general(low_sel, cpad[...], NT, preferred_element_type=F32).astype(BF)
+    hub[0, 2 * PTS :, :] = lax.dot_general(low_sel, cpad[...], NT, preferred_element_type=F32).astype(BF)
+    pl.semaphore_wait(barrier, 67 - jnp.where(self_step(), 1, 0))
+
+    def s_copy(n):
+        return remote(hub.at[0], hub.at[n], s_ssem.at[n], s_rsem.at[n], 2 * around(z + HUBS[n]) + ylo, col)
+
+    for n in (3, 4, 1, 2):
+        s_copy(n).start()
+
+    def a_copy(m, y):
+        n, d = SECOND[m]
+        plane = around(z - HUBS[n])
+        return remote(
+            hub.at[n], got.at[ylo, col], a_ssem.at[m, y], a_rsem.at[ylo, col], 2 * around(z + d) + y, plane
+        )
+
+    def a_to_self(m, y):
+        n, d = SECOND[m]
+        return (around(z - HUBS[n]) == col) & (ylo == y) if d == 0 else None
+
+    def a_start(n):
+        for m in range(len(SECOND)):
+            if SECOND[m][0] == n:
+                for y in range(2):
+                    own = a_to_self(m, y)
+                    if own is None:
+                        a_copy(m, y).start()
+                    else:
+                        @pl.when(jnp.logical_not(own))
+                        def _(m=m, y=y):
+                            a_copy(m, y).start()
+
+        @pl.when(around(z - HUBS[n]) == col)
+        def _():
+            got[pl.ds(ylo, 1), pl.ds(col, 1)] = hub[n].reshape(1, 1, 80, 128)
+
+    a_start(0)
+
     tail = jnp.dot(val, onehot((bands == lanes + 896) & (lanes < 104)), preferred_element_type=F32)
     tail = tail + jnp.dot(con, onehot((bands + 104 == lanes) & (bands < NCW)), preferred_element_type=F32)
     g_all[pl.ds(col, 1), :, 0:896] = val[:, 0:896].reshape(1, PTS, 896)
     g_all[pl.ds(col, 1), :, 896:NBP] = tail.astype(BF).reshape(1, PTS, 128)
 
-    w_local.wait()
-    b_local.wait()
-    same = jnp.where(col == z, 2, 0)
-    pl.semaphore_wait(barrier, 64 - same)
-
-    def a_copy(i):
-        return remote(blk, got.at[col], a_ssem.at[i], a_rsem.at[col], 2 * i + ylo, z)
-
-    def a_start(i, _):
-        there = lax.rem(z + 8 + i, NZ)
-
-        @pl.when((there != z) | (col != z))
-        def _():
-            a_copy(there).start()
-
-        return 0
-
-    lax.fori_loop(0, NZ, a_start, 0)
-
-    @pl.when(col == z)
-    def _():
-        got[pl.ds(col, 1)] = blk[...].reshape(1, 80, 128)
-
-    w_copy = remote(w_ref, w_all.at[core], wb_ssem.at[0], wb_rsem.at[0], row, mate)
-    b_copy = remote(b_ref, b_all.at[core], wb_ssem.at[1], wb_rsem.at[1], row, mate)
-    w_copy.start()
-    b_copy.start()
-
     def g_copy(k):
         return remote(g_all.at[col], g_all.at[col], g_ssem.at[k], g_rsem.at[chip], row, 2 * k + core)
 
@@ -148,38 +175,35 @@
 
     h_copy(chip, core).start()
 
-    def a_recv(i, _):
-        @pl.when((i != col) | (col != z))
-        def _():
-            remote(blk, got.at[i], a_ssem.at[i], a_rsem.at[i], row, mate).wait_recv()
-
-        return 0
-
-    lax.fori_loop(0, NCOL, a_recv, 0)
-
-    def pick_own(i, _):
-        picks[core, ylo, pl.ds(i, 1)] = got[pl.ds(i, 1), pl.ds(pl.multiple_of(core * PTS, PTS), PTS), :]
-        return 0
-
-    lax.fori_loop(0, NCOL, pick_own, 0)
-    for g in range(4):
-        part = got[4 * g, 64:80, :].astype(F32)
-        for s in range(1, 4):
-            part = part + got[4 * g + s, 64:80, :].astype(F32)
-        lows[core, ylo, :, g * 128 : (g + 1) * 128] = part.astype(BF)
-
-    there_half = got.at[:, pl.ds(pl.multiple_of((1 - core) * PTS, PTS), PTS), :]
-    own_half = picks.at[core, ylo]
-    own_low = lows.at[core, ylo]
-    slot = core * 2 + ylo
+    w_copy = remote(w_ref, w_all.at[1], wb_ssem.at[0], wb_rsem.at[0], row, mate)
+    b_copy = remote(b_ref, b_all.at[1], wb_ssem.at[1], wb_rsem.at[1], row, mate)
+    w_copy.start()
+    b_copy.start()
+
+    for n in (1, 2, 3, 4):
+        s_copy(n).wait_recv()
+        a_start(n)
+
     passes = []
-    for n, (src, prow, pcol) in enumerate(
-        ((there_half, row, mate), (own_half, other_row, col), (there_half, other_row, mate))
-    ):
-        passes.append(remote(src, picks.at[core, ylo], f_ssem.at[0, n], f_rsem.at[0, slot], prow, pcol))
-        passes.append(remote(own_low, lows.at[core, ylo], f_ssem.at[1, n], f_rsem.at[1, slot], prow, pcol))
-    for copy in passes:
-        copy.start()
+    for y in range(2):
+        def a_recv(i, _, y=y):
+            @pl.when((2 * hub_z + y != row) | (i != col))
+            def _():
+                remote(hub.at[0], got.at[y, i], a_ssem.at[0, 0], a_rsem.at[y, i], row, mate).wait_recv()
+
+            return 0
+
+        lax.fori_loop(0, NCOL, a_recv, 0)
+        for g in range(4):
+            part = got[y, 4 * g, 64:80, :].astype(F32)
+            for s in range(1, 4):
+                part = part + got[y, 4 * g + s, 64:80, :].astype(F32)
+            lows[0, y, :, g * 128 : (g + 1) * 128] = part.astype(BF)
+        half = got.at[y, :, pl.ds(pl.multiple_of((1 - core) * PTS, PTS), PTS), :]
+        passes.append(remote(half, picks.at[y], f_ssem.at[0, y], f_rsem.at[0, y], row, mate))
+        passes.append(remote(lows.at[0, y], lows.at[1, y], f_ssem.at[1, y], f_rsem.at[1, y], row, mate))
+        passes[-2].start()
+        passes[-1].start()
 
     def h_start(i, _):
         k = lax.rem(chip + i, 8)
@@ -189,21 +213,20 @@
 
     lax.fori_loop(1, 8, h_start, 0)
 
+    eye = onehot(iota((128, 128), 0) == iota((128, 128), 1))
+    own_rows = pl.ds(pl.multiple_of(core * PTS, PTS), PTS)
     for n in range(4):
-        @pl.when(slot != n)
-        def _(n=n):
-            a, b = n // 2, n % 2
-            remote(own_half, picks.at[a, b], f_ssem.at[0, 0], f_rsem.at[0, n], row, mate).wait_recv()
-            remote(own_low, lows.at[a, b], f_ssem.at[1, 0], f_rsem.at[1, n], row, mate).wait_recv()
-
-    eye = onehot(iota((128, 128), 0) == iota((128, 128), 1))
-    for n in range(4):
-        a, b = n // 2, n % 2
-        turned[:, n * ROWS : (n + 1) * ROWS] = lax.dot_general(
-            eye, picks[a, b].reshape(ROWS, 128), NT, preferred_element_type=F32
-        )
-        low_f32[:, n * ROWS : (n + 1) * ROWS] = lows[a, b].astype(F32)
-
+        a, y = n // 2, n % 2
+        span = slice(n * ROWS, (n + 1) * ROWS)
+        if a:
+            passes[2 * y].wait_recv()
+            passes[2 * y + 1].wait_recv()
+        half = picks[y] if a else got[y, :, own_rows, :]
+        turned[:, span] = lax.dot_general(eye, half.reshape(ROWS, 128), NT, preferred_element_type=F32)
+        low_f32[:, span] = lows[a, y].astype(F32)
+
+    loads[4].wait()
+    loads[5].wait()
     w_copy.wait_recv()
     b_copy.wait_recv()
     left_e[...] = (turned[0:64, :] * turned[64:128, :]).astype(BF)
@@ -273,10 +296,8 @@
 
     lax.fori_loop(0, 8, h_wait, 0)
     points = g_all[...].reshape(ROWS, NBP)
-    mine = jnp.zeros((8, NBP), jnp.int32)
-    for i in range(8):
-        mine = jnp.where(iota((8, NBP), 0) == i, pvs_ref[col * 8 + i], mine)
-    sel = onehot(mine == iota((8, NBP), 1))
+    mine = jnp.where(iota((8, 128), 1) == col * 8 + iota((8, 128), 0), pv_ref[...].astype(F32), 0.0)
+    sel = onehot(jnp.sum(mine, axis=1, keepdims=True) == iota((8, NBP), 1).astype(F32))
     vpt = lax.dot_general(sel, points, NT, preferred_element_type=F32)
     sel = onehot((iota((16, NBP), 1) == iota((16, NBP), 0) + NB) & (iota((16, NBP), 0) < NCW))
     low_f32[:, 0:ROWS] = lax.dot_general(sel, points, NT, preferred_element_type=F32)
@@ -357,10 +378,6 @@
     y_copy.start()
 
     def drain(i, _):
-        @pl.when((i != z) | (col != z))
-        def _():
-            a_copy(i).wait_send()
-
         @pl.when(i != z)
         def _():
             c_copy(i).wait_send()
@@ -368,6 +385,17 @@
         return 0
 
     lax.fori_loop(0, NZ, drain, 0)
+    for n in range(1, 5):
+        s_copy(n).wait_send()
+    for m in range(len(SECOND)):
+        for y in range(2):
+            own = a_to_self(m, y)
+            if own is None:
+                a_copy(m, y).wait_send()
+            else:
+                @pl.when(jnp.logical_not(own))
+                def _(m=m, y=y):
+                    a_copy(m, y).wait_send()
 
     def drain8(i, _):
         @pl.when(i != chip)
@@ -399,14 +427,18 @@
     out = pl.pallas_call(
         kernel,
         out_shape=jax.ShapeDtypeStruct((8, SEGP), F32),
-        in_specs=[vmem, vmem, vmem, vmem, pl.BlockSpec(memory_space=pltpu.SMEM), hbm, hbm],
+        in_specs=[hbm] * 6,
         out_specs=vmem,
         scratch_shapes=[
-            pltpu.VMEM((80, 128), BF),
+            pltpu.VMEM((PTS, NB), BF),
+            pltpu.VMEM((PTS, NB), BF),
+            pltpu.VMEM((1, 128), jnp.int32),
+            pltpu.VMEM((1, 128), jnp.int32),
+            pltpu.VMEM((5, 80, 128), BF),
             pltpu.VMEM((128, NB), BF),
             pltpu.VMEM((NCOL, PTS, NBP), BF),
-            pltpu.VMEM((NCOL, 80, 128), BF),
-            pltpu.VMEM((2, 2, NCOL, PTS, 128), BF),
+            pltpu.VMEM((2, NCOL, 80, 128), BF),
+            pltpu.VMEM((2, NCOL, PTS, 128), BF),
             pltpu.VMEM((2, 2, 16, ROWS), BF),
             pltpu.VMEM((16, 2 * COLS), F32),
             pltpu.VMEM((128, 2 * COLS), F32),
@@ -423,23 +455,24 @@
             pltpu.VMEM((NZ, 16, SEGP), BF),
             pltpu.VMEM((2, 8, SEGP), F32),
             pltpu.VMEM((8, SEGP), F32),
-            dma((2,)),
+            dma((6,)),
             dma((2,)), dma((2,)),
-            dma((16,)), dma((16,)),
+            dma((len(SECOND), 2)), dma((2, 16)),
+            dma((5,)), dma((5,)),
             dma((8,)), dma((8,)),
             dma((8,)), dma((8,)),
-            dma((2, 3)), dma((2, 4)),
+            dma((2, 2)), dma((2, 2)),
             dma((2, 8)), dma((2, 8)),
             dma((16,)), dma((16,)),
             dma, dma,
         ],
         compiler_params=pltpu.CompilerParams(
-            collective_id=0, has_side_effects=True, vmem_limit_bytes=48 * 2**20
+            collective_id=0, has_side_effects=True, vmem_limit_bytes=60 * 2**20
         ),
         name="kernel_panel",
     )(
         orb_valence, orb_conduction, panel_valence.reshape(1, -1), panel_conduction.reshape(1, -1),
-        panel_valence, screened, bare,
+        screened, bare,
     )
     return out[:, :SEG].T
 

time: 80.5 us -> 65.1 us (0.81); the launches traced: 79 us -> 64.9 us
  Pallas kernels: 73.6 us -> 63.6 us
  local copies, waits for them, and re-layouts: 5.4 us -> 1.31 us
    pallas_call x1, Pallas kernels: 73.6 us -> 63.6 us  [body(): pl.pallas_call(kernel, out_shape=jax.ShapeDtypeStruct((8, SEGP), F32), in...]
    unnamed x12 -> x0, local copies, waits for them, and re-layouts: 4.8 us -> none
where the time goes in v2:
time: 65.1 us; the launch traced here: 64.9 us
  Pallas kernels  63.6 us (98%)
  local copies, waits for them, and re-layouts  1.31 us (2%)
    pallas_call x1, Pallas kernels, body(): pl.pallas_call(kernel, out_shape=jax.ShapeDtypeStruct((8, SEGP), F32), in...  63.6 us
    transpose x1, local copies, waits for them, and re-layouts, body(): return out[:, :SEG].T  1.31 us

profile of v2, /device:TPU:1, one launch (start us, length us, event | category | flops | bytes accessed | tf_op | source)
XLA Modules:
  0.0 64.9 jit_solution(8783655146575777922)
XLA Ops:
  0.0 63.6 %kernel_panel.1 = f32[8,384]{1,0:T(8,128)} custom-call(bf16[32,1000]{1,0:T(8,128)(2,1)} %v_hbm.1, bf16[32,1000]{1,0:T(8,128)(2,1)} %c_hbm.1, s32[1,128]{1,0:T(1,128)} %bitcast.4, s32[1,128]{1,0:T(1,128)} %bitcast.5, bf16[512,1024]{1,0:T(8,128)(2,1)} %w_ref.1, bf16[512,1024]{1,0:T(8,128)(2,1)} %b_ref.1), custom_call_target="tpu_custom_call" | custom-call | tf_op jit(solution)/shard_map/kernel_panel/pallas_call | solution.py:427
  63.6 1.3 %slice_bitcast_fusion = f32[375,8]{0,1:T(8,128)} fusion(f32[8,384]{1,0:T(8,128)} %kernel_panel.1), kind=kLoop, calls=%fused_computation | loop fusion | bytes 24000 | tf_op jit(solution)/shard_map/transpose | solution.py:477

commit v3 on v2

--- a/solution.py
+++ b/solution.py
@@ -35,7 +35,7 @@
 def kernel(
     v_hbm, c_hbm, pv_hbm, pc_hbm, w_ref, b_ref, out_ref,
     v_ref, c_ref, pv_ref, pc_ref,
-    hub, cpad, g_all, got, picks, lows, low_f32, turned, left, left_e,
+    hub, cpad, g_all, swap_out, swap_in, got, low_f32, turned, left, left_e,
     w_all, b_all, send0, send1, recv0, recv1, panel, seg_out, seg_in, total, y_in,
     loc_sem, wb_ssem, wb_rsem, a_ssem, a_rsem, s_ssem, s_rsem, g_ssem, g_rsem, h_ssem, h_rsem,
     f_ssem, f_rsem, b_ssem, b_rsem, c_ssem, c_rsem, y_ssem, y_rsem,
@@ -61,7 +61,7 @@
     loads = [
         pltpu.make_async_copy(src, dst, loc_sem.at[n])
         for n, (src, dst) in enumerate(
-            ((c_hbm, c_ref), (pc_hbm, pc_ref), (v_hbm, v_ref), (pv_hbm, pv_ref), (w_ref, w_all.at[0]), (b_ref, b_all.at[0]))
+            ((c_hbm, c_ref), (pc_hbm, pc_ref), (v_hbm, v_ref), (pv_hbm, pv_ref), (w_ref, w_all.at[core]), (b_ref, b_all.at[core]))
         )
     ]
     for copy in loads:
@@ -72,20 +72,25 @@
     def greet(prow, pcol):
         pl.semaphore_signal(barrier, inc=1, device_id={"prow": prow, "pcol": pcol}, device_id_type=MESH)
 
-    ahead = around(z - col)
-    step = jnp.where(ahead == 8, 2, lax.rem(ahead + 1, 3) - 1)
-    step = jnp.where(ahead > 8, 1 - lax.rem(17 - ahead, 3), step)
-    hub_z = around(z - step)
-
-    def self_step():
-        return hub_z == z
+    def step_of(plane):
+        ahead = around(z - plane)
+        back = 1 - lax.rem(17 - ahead, 3)
+        return jnp.where(ahead > 8, back, jnp.where(ahead == 8, 2, lax.rem(ahead + 1, 3) - 1))
+
+    hub_z = [around(z - step_of(2 * chip + e)) for e in range(2)]
 
     def greet_step(i, _):
-        for y in range(2):
-            @pl.when((2 * hub_z + y != row) | (i != col))
-            def _(y=y):
-                greet(2 * hub_z + y, i)
-
+        for e in range(2):
+            for y in range(2):
+                @pl.when((hub_z[e] != z) | (ylo != y) | (i != chip))
+                def _(e=e, y=y):
+                    greet(2 * hub_z[e] + y, 2 * i + core)
+
+        return 0
+
+    lax.fori_loop(0, 8, greet_step, 0)
+
+    def greet_line(i, _):
         @pl.when(i != col)
         def _():
             greet(row, i)
@@ -96,7 +101,7 @@
 
         return 0
 
-    lax.fori_loop(0, NZ, greet_step, 0)
+    lax.fori_loop(0, NZ, greet_line, 0)
     for n in range(1, 5):
         greet(2 * around(z - HUBS[n]) + ylo, col)
     greet(other_row, col)
@@ -110,14 +115,45 @@
     vp = jnp.dot(val, onehot(bands == pv_ref[...]), preferred_element_type=F32)
     cp = jnp.dot(con, onehot(bands == pc_ref[...]), preferred_element_type=F32)
     lane = iota((PTS, 128), 1)
-    hub[0, 0:PTS, :] = jnp.where(lane < 64, cp, pltpu.roll(vp, 64, 1)).astype(BF)
-    hub[0, PTS : 2 * PTS, :] = jnp.where(lane < 64, pltpu.roll(cp, 64, 1), vp).astype(BF)
+    first = jnp.where(lane < 64, cp, pltpu.roll(vp, 64, 1))
+    second = jnp.where(lane < 64, pltpu.roll(cp, 64, 1), vp)
     cpad[...] = jnp.zeros((128, NB), BF)
     cpad[pl.ds(pl.multiple_of(lax.rem(col, 4) * PTS, PTS), PTS), :] = con
     low_rows = iota((16, NB), 0)
     low_sel = onehot((low_rows == iota((16, NB), 1)) & (low_rows < NCW))
-    hub[0, 2 * PTS :, :] = lax.dot_general(low_sel, cpad[...], NT, preferred_element_type=F32).astype(BF)
-    pl.semaphore_wait(barrier, 67 - jnp.where(self_step(), 1, 0))
+    low = lax.dot_general(low_sel, cpad[...], NT, preferred_element_type=F32)
+    swap_out[0:PTS, :] = jnp.where(core == 0, second, first).astype(BF)
+    swap_out[PTS:, :] = low.astype(BF)
+    own_pts = pl.ds(pl.multiple_of(core * PTS, PTS), PTS)
+    mate_pts = pl.ds(pl.multiple_of((1 - core) * PTS, PTS), PTS)
+    hub[0, own_pts, :] = jnp.where(core == 0, first, second).astype(BF)
+    tail = jnp.dot(val, onehot((bands == lanes + 896) & (lanes < 104)), preferred_element_type=F32)
+    tail = tail + jnp.dot(con, onehot((bands + 104 == lanes) & (bands < NCW)), preferred_element_type=F32)
+    g_all[pl.ds(col, 1), :, 0:896] = val[:, 0:896].reshape(1, PTS, 896)
+    g_all[pl.ds(col, 1), :, 896:NBP] = tail.astype(BF).reshape(1, PTS, 128)
+
+    pl.semaphore_wait(barrier, 67 - jnp.where((hub_z[0] == z) | (hub_z[1] == z), 1, 0))
+    def g_copy(k):
+        return remote(g_all.at[col], g_all.at[col], g_ssem.at[k], g_rsem.at[chip], row, 2 * k + core)
+
+    def g_start(i, _):
+        there = lax.rem(chip + i, 8)
+        g_copy(there).start()
+        return 0
+
+    lax.fori_loop(1, 8, g_start, 0)
+
+    def h_copy(k, mine):
+        slot = 2 * k + mine
+        return remote(g_all.at[slot], g_all.at[slot], h_ssem.at[k], h_rsem.at[k], row, mate)
+
+    h_copy(chip, core).start()
+
+    swap = remote(swap_out, swap_in, f_ssem, f_rsem, row, mate)
+    swap.start()
+    swap.wait_recv()
+    hub[0, mate_pts, :] = swap_in[0:PTS, :]
+    hub[0, 2 * PTS :, :] = (low + swap_in[PTS:, :].astype(F32)).astype(BF)
 
     def s_copy(n):
         return remote(hub.at[0], hub.at[n], s_ssem.at[n], s_rsem.at[n], 2 * around(z + HUBS[n]) + ylo, col)
@@ -129,12 +165,16 @@
         n, d = SECOND[m]
         plane = around(z - HUBS[n])
         return remote(
-            hub.at[n], got.at[ylo, col], a_ssem.at[m, y], a_rsem.at[ylo, col], 2 * around(z + d) + y, plane
+            hub.at[n], got.at[lax.rem(plane, 2), ylo, chip], a_ssem.at[m, y], a_rsem.at[lax.rem(plane, 2), ylo, chip],
+            2 * around(z + d) + y, 2 * lax.div(plane, 2) + core,
         )
+
+    def own_plane(n):
+        return lax.div(around(z - HUBS[n]), 2) == chip
 
     def a_to_self(m, y):
         n, d = SECOND[m]
-        return (around(z - HUBS[n]) == col) & (ylo == y) if d == 0 else None
+        return own_plane(n) & (ylo == y) if d == 0 else None
 
     def a_start(n):
         for m in range(len(SECOND)):
@@ -148,35 +188,14 @@
                         def _(m=m, y=y):
                             a_copy(m, y).start()
 
-        @pl.when(around(z - HUBS[n]) == col)
-        def _():
-            got[pl.ds(ylo, 1), pl.ds(col, 1)] = hub[n].reshape(1, 1, 80, 128)
+        @pl.when(own_plane(n))
+        def _():
+            got[lax.rem(around(z - HUBS[n]), 2), ylo, chip] = hub[n]
 
     a_start(0)
 
-    tail = jnp.dot(val, onehot((bands == lanes + 896) & (lanes < 104)), preferred_element_type=F32)
-    tail = tail + jnp.dot(con, onehot((bands + 104 == lanes) & (bands < NCW)), preferred_element_type=F32)
-    g_all[pl.ds(col, 1), :, 0:896] = val[:, 0:896].reshape(1, PTS, 896)
-    g_all[pl.ds(col, 1), :, 896:NBP] = tail.astype(BF).reshape(1, PTS, 128)
-
-    def g_copy(k):
-        return remote(g_all.at[col], g_all.at[col], g_ssem.at[k], g_rsem.at[chip], row, 2 * k + core)
-
-    def g_start(i, _):
-        there = lax.rem(chip + i, 8)
-        g_copy(there).start()
-        return 0
-
-    lax.fori_loop(1, 8, g_start, 0)
-
-    def h_copy(k, mine):
-        slot = 2 * k + mine
-        return remote(g_all.at[slot], g_all.at[slot], h_ssem.at[k], h_rsem.at[k], row, mate)
-
-    h_copy(chip, core).start()
-
-    w_copy = remote(w_ref, w_all.at[1], wb_ssem.at[0], wb_rsem.at[0], row, mate)
-    b_copy = remote(b_ref, b_all.at[1], wb_ssem.at[1], wb_rsem.at[1], row, mate)
+    w_copy = remote(w_ref, w_all.at[core], wb_ssem.at[0], wb_rsem.at[0], row, mate)
+    b_copy = remote(b_ref, b_all.at[core], wb_ssem.at[1], wb_rsem.at[1], row, mate)
     w_copy.start()
     b_copy.start()
 
@@ -184,46 +203,31 @@
         s_copy(n).wait_recv()
         a_start(n)
 
-    passes = []
-    for y in range(2):
-        def a_recv(i, _, y=y):
-            @pl.when((2 * hub_z + y != row) | (i != col))
+    eye = onehot(iota((128, 128), 0) == iota((128, 128), 1))
+
+    def arrive(e, y):
+        def a_recv(i, _):
+            @pl.when((hub_z[e] != z) | (ylo != y) | (i != chip))
             def _():
-                remote(hub.at[0], got.at[y, i], a_ssem.at[0, 0], a_rsem.at[y, i], row, mate).wait_recv()
+                remote(hub.at[0], got.at[e, y, i], a_ssem.at[0, 0], a_rsem.at[e, y, i], row, mate).wait_recv()
 
             return 0
 
-        lax.fori_loop(0, NCOL, a_recv, 0)
-        for g in range(4):
-            part = got[y, 4 * g, 64:80, :].astype(F32)
-            for s in range(1, 4):
-                part = part + got[y, 4 * g + s, 64:80, :].astype(F32)
-            lows[0, y, :, g * 128 : (g + 1) * 128] = part.astype(BF)
-        half = got.at[y, :, pl.ds(pl.multiple_of((1 - core) * PTS, PTS), PTS), :]
-        passes.append(remote(half, picks.at[y], f_ssem.at[0, y], f_rsem.at[0, y], row, mate))
-        passes.append(remote(lows.at[0, y], lows.at[1, y], f_ssem.at[1, y], f_rsem.at[1, y], row, mate))
-        passes[-2].start()
-        passes[-1].start()
-
-    def h_start(i, _):
-        k = lax.rem(chip + i, 8)
-        remote(g_all.at[col], g_all.at[2 * k + core], g_ssem.at[k], g_rsem.at[k], row, mate).wait_recv()
-        h_copy(k, core).start()
-        return 0
-
-    lax.fori_loop(1, 8, h_start, 0)
-
-    eye = onehot(iota((128, 128), 0) == iota((128, 128), 1))
-    own_rows = pl.ds(pl.multiple_of(core * PTS, PTS), PTS)
-    for n in range(4):
-        a, y = n // 2, n % 2
-        span = slice(n * ROWS, (n + 1) * ROWS)
-        if a:
-            passes[2 * y].wait_recv()
-            passes[2 * y + 1].wait_recv()
-        half = picks[y] if a else got[y, :, own_rows, :]
-        turned[:, span] = lax.dot_general(eye, half.reshape(ROWS, 128), NT, preferred_element_type=F32)
-        low_f32[:, span] = lows[a, y].astype(F32)
+        lax.fori_loop(0, 8, a_recv, 0)
+
+    for e in range(2):
+        for y in range(2):
+            arrive(e, y)
+
+    for e in range(2):
+        for y in range(2):
+            at = (2 * e + y) * ROWS
+            rows = got[e, y, :, 0:64, :].reshape(ROWS, 128)
+            turned[:, at : at + ROWS] = lax.dot_general(eye, rows, NT, preferred_element_type=F32)
+            for g in range(4):
+                low_f32[:, at + g * 128 : at + g * 128 + 128] = (
+                    got[e, y, 2 * g, 64:80, :].astype(F32) + got[e, y, 2 * g + 1, 64:80, :].astype(F32)
+                )
 
     loads[4].wait()
     loads[5].wait()
@@ -237,15 +241,20 @@
             lhs[:, COLS:], rhs[1, rows, :], NT, preferred_element_type=F32
         )
 
-    far = 1 - lax.div(z, 8)
-
-    def build(half):
+    def band_of(parity, i):
+        return 3 * parity + i + 3 * (i // 3)
+
+    def plane_of(parity, i):
+        return 4 * parity + i + 4 * lax.div(i, 4)
+
+    near = lax.rem(lax.div(z, 4), 2)
+
+    def build(parity):
         def step(m, _):
             tile = turned[pl.ds(pl.multiple_of(m * 8, 8), 8), :]
             for p in range(HALF // 2):
-                first = half * HALF + 2 * p
                 pair = jnp.concatenate(
-                    [tile * low_f32[pl.ds(first, 1), :], tile * low_f32[pl.ds(first + 1, 1), :]], axis=0
+                    [tile * low_f32[pl.ds(band_of(parity, 2 * p + k), 1), :] for k in range(2)], axis=0
                 )
                 left[pl.ds(pl.multiple_of(m * 48 + 16 * p, 16), 16), :] = pair.astype(BF)
             return 0
@@ -256,7 +265,7 @@
         sends, recvs = ((send0, recv0), (send1, recv1))[n]
         return remote(sends.at[m], recvs.at[chip], b_ssem.at[n, m], b_rsem.at[n, chip], row, 8 * core + m)
 
-    order = (far, 1 - far)
+    order = (near, 1 - near)
     for n in range(2):
         sends, recvs = ((send0, recv0), (send1, recv1))[n]
         build(order[n])
@@ -290,6 +299,14 @@
 
         lax.fori_loop(0, 8, b_start, 0)
 
+    def h_start(i, _):
+        k = lax.rem(chip + i, 8)
+        remote(g_all.at[col], g_all.at[2 * k + core], g_ssem.at[k], g_rsem.at[k], row, mate).wait_recv()
+        h_copy(k, core).start()
+        return 0
+
+    lax.fori_loop(1, 8, h_start, 0)
+
     def h_wait(i, _):
         h_copy(i, 1 - core).wait_recv()
         return 0
@@ -320,7 +337,7 @@
     lane = iota((8, SEGP), 1)
     for n in range(2):
         recvs = (recv0, recv1)[n]
-        half = order[n]
+        parity = order[n]
         b_recv(n)
         d = recvs[0].astype(F32)
         for k in range(1, 8):
@@ -328,7 +345,7 @@
         if n == 0:
             exch = 2.0 * (d[48:56] + d[56:64])
         comb = [
-            low_f32[pl.ds(half * HALF + i, 1), 0:ROWS] * exch - vpt * d[i * 8 : i * 8 + 8] for i in range(HALF)
+            low_f32[pl.ds(band_of(parity, i), 1), 0:ROWS] * exch - vpt * d[i * 8 : i * 8 + 8] for i in range(HALF)
         ]
         comb = jnp.concatenate(comb, axis=0).astype(BF)
         panel[...] = jnp.dot(comb, points, preferred_element_type=F32)
@@ -345,10 +362,10 @@
                     more = pltpu.roll(panel[band0 * 8 + 8 : band0 * 8 + 16, :], NB - off, 1)[:, 0:SEGP]
                     seg = jnp.where(lane < NB - off, seg, more)
                 halves.append(seg)
-            seg_out[pl.ds(half * 8 + zl, 1)] = jnp.concatenate(halves, axis=0).astype(BF).reshape(1, 16, SEGP)
-
-        def c_start(i, _, half=half):
-            there = half * 8 + i
+            seg_out[pl.ds(plane_of(parity, zl), 1)] = jnp.concatenate(halves, axis=0).astype(BF).reshape(1, 16, SEGP)
+
+        def c_start(i, _, parity=parity):
+            there = plane_of(parity, i)
 
             @pl.when(there != z)
             def _():
@@ -412,8 +429,7 @@
         return 0
 
     lax.fori_loop(0, 8, drain8, 0)
-    for copy in passes:
-        copy.wait_send()
+    swap.wait_send()
     w_copy.wait_send()
     b_copy.wait_send()
     y_copy.wait()
@@ -437,9 +453,9 @@
             pltpu.VMEM((5, 80, 128), BF),
             pltpu.VMEM((128, NB), BF),
             pltpu.VMEM((NCOL, PTS, NBP), BF),
-            pltpu.VMEM((2, NCOL, 80, 128), BF),
-            pltpu.VMEM((2, NCOL, PTS, 128), BF),
-            pltpu.VMEM((2, 2, 16, ROWS), BF),
+            pltpu.VMEM((48, 128), BF),
+            pltpu.VMEM((48, 128), BF),
+            pltpu.VMEM((2, 2, 8, 80, 128), BF),
             pltpu.VMEM((16, 2 * COLS), F32),
             pltpu.VMEM((128, 2 * COLS), F32),
             pltpu.VMEM((8 * HALF * 8, 2 * COLS), BF),
@@ -457,11 +473,11 @@
             pltpu.VMEM((8, SEGP), F32),
             dma((6,)),
             dma((2,)), dma((2,)),
-            dma((len(SECOND), 2)), dma((2, 16)),
+            dma((len(SECOND), 2)), dma((2, 2, 8)),
             dma((5,)), dma((5,)),
             dma((8,)), dma((8,)),
             dma((8,)), dma((8,)),
-            dma((2, 2)), dma((2, 2)),
+            dma, dma,
             dma((2, 8)), dma((2, 8)),
             dma((16,)), dma((16,)),
             dma, dma,

time: 65.1 us -> 64.4 us (0.989)
  no operation moved by 1% of the time
where the time goes in v3:
time: 64.4 us; the launch traced here: 64.3 us
  Pallas kernels  63 us (98%)
  local copies, waits for them, and re-layouts  1.31 us (2%)
    pallas_call x1, Pallas kernels, body(): pl.pallas_call(kernel, out_shape=jax.ShapeDtypeStruct((8, SEGP), F32), in...  63 us
    transpose x1, local copies, waits for them, and re-layouts, body(): return out[:, :SEG].T  1.31 us

profile of v3, /device:TPU:1, one launch (start us, length us, event | category | flops | bytes accessed | tf_op | source)
XLA Modules:
  0.0 64.3 jit_solution(14802485627180287612)
XLA Ops:
  0.0 63.0 %kernel_panel.1 = f32[8,384]{1,0:T(8,128)} custom-call(bf16[32,1000]{1,0:T(8,128)(2,1)} %v_hbm.1, bf16[32,1000]{1,0:T(8,128)(2,1)} %c_hbm.1, s32[1,128]{1,0:T(1,128)} %bitcast.4, s32[1,128]{1,0:T(1,128)} %bitcast.5, bf16[512,1024]{1,0:T(8,128)(2,1)} %w_ref.1, bf16[512,1024]{1,0:T(8,128)(2,1)} %b_ref.1), custom_call_target="tpu_custom_call" | custom-call | tf_op jit(solution)/shard_map/kernel_panel/pallas_call | solution.py:443
  63.0 1.3 %slice_bitcast_fusion = f32[375,8]{0,1:T(8,128)} fusion(f32[8,384]{1,0:T(8,128)} %kernel_panel.1), kind=kLoop, calls=%fused_computation | loop fusion | bytes 24000 | tf_op jit(solution)/shard_map/transpose | solution.py:493

commit v4 on v3

--- a/solution.py
+++ b/solution.py
@@ -36,7 +36,7 @@
     v_hbm, c_hbm, pv_hbm, pc_hbm, w_ref, b_ref, out_ref,
     v_ref, c_ref, pv_ref, pc_ref,
     hub, cpad, g_all, swap_out, swap_in, got, low_f32, turned, left, left_e,
-    w_all, b_all, send0, send1, recv0, recv1, panel, seg_out, seg_in, total, y_in,
+    w_all, b_all, w_turned, b_turned, send0, send1, recv0, recv1, panel, seg_out, seg_in, total, y_in,
     loc_sem, wb_ssem, wb_rsem, a_ssem, a_rsem, s_ssem, s_rsem, g_ssem, g_rsem, h_ssem, h_rsem,
     f_ssem, f_rsem, b_ssem, b_rsem, c_ssem, c_rsem, y_ssem, y_rsem,
 ):
@@ -79,6 +79,10 @@
 
     hub_z = [around(z - step_of(2 * chip + e)) for e in range(2)]
 
+    for n in (4, 3, 2, 1):
+        greet(2 * around(z - HUBS[n]) + ylo, col)
+    greet(other_row, col)
+
     def greet_step(i, _):
         for e in range(2):
             for y in range(2):
@@ -95,16 +99,9 @@
         def _():
             greet(row, i)
 
-        @pl.when(i != z)
-        def _():
-            greet(2 * i + ylo, col)
-
         return 0
 
     lax.fori_loop(0, NZ, greet_line, 0)
-    for n in range(1, 5):
-        greet(2 * around(z - HUBS[n]) + ylo, col)
-    greet(other_row, col)
 
     for copy in loads[:4]:
         copy.wait()
@@ -132,7 +129,7 @@
     g_all[pl.ds(col, 1), :, 0:896] = val[:, 0:896].reshape(1, PTS, 896)
     g_all[pl.ds(col, 1), :, 896:NBP] = tail.astype(BF).reshape(1, PTS, 128)
 
-    pl.semaphore_wait(barrier, 67 - jnp.where((hub_z[0] == z) | (hub_z[1] == z), 1, 0))
+    pl.semaphore_wait(barrier, 52 - jnp.where((hub_z[0] == z) | (hub_z[1] == z), 1, 0))
     def g_copy(k):
         return remote(g_all.at[col], g_all.at[col], g_ssem.at[k], g_rsem.at[chip], row, 2 * k + core)
 
@@ -203,6 +200,21 @@
         s_copy(n).wait_recv()
         a_start(n)
 
+    loads[4].wait()
+    loads[5].wait()
+    w_copy.wait_recv()
+    b_copy.wait_recv()
+
+    def turn(i, _):
+        e, t = lax.div(i, 4), lax.rem(i, 4)
+        span = pl.ds(pl.multiple_of(t * 256, 256), 256)
+        rows = pl.ds(pl.multiple_of(e * COLS + t * 256, 256), 256)
+        w_turned[rows, :] = w_all[e, :, span].T
+        b_turned[rows, :] = b_all[e, :, span].T
+        return 0
+
+    lax.fori_loop(0, 8, turn, 0)
+
     eye = onehot(iota((128, 128), 0) == iota((128, 128), 1))
 
     def arrive(e, y):
@@ -229,17 +241,10 @@
                     got[e, y, 2 * g, 64:80, :].astype(F32) + got[e, y, 2 * g + 1, 64:80, :].astype(F32)
                 )
 
-    loads[4].wait()
-    loads[5].wait()
-    w_copy.wait_recv()
-    b_copy.wait_recv()
     left_e[...] = (turned[0:64, :] * turned[64:128, :]).astype(BF)
 
-    def against(lhs, rhs, n):
-        rows = pl.ds(pl.multiple_of(n * 256, 256), 256)
-        return lax.dot_general(lhs[:, 0:COLS], rhs[0, rows, :], NT, preferred_element_type=F32) + lax.dot_general(
-            lhs[:, COLS:], rhs[1, rows, :], NT, preferred_element_type=F32
-        )
+    def against(lhs, rhs, span):
+        return jnp.dot(lhs[...], rhs[:, span], preferred_element_type=F32)
 
     def band_of(parity, i):
         return 3 * parity + i + 3 * (i // 3)
@@ -272,11 +277,11 @@
 
         def mul(t, _, n=n, sends=sends):
             span = pl.ds(pl.multiple_of(t * 256, 256), 256)
-            d = against(left[...], w_all, t).astype(BF)
+            d = against(left, w_turned, span).astype(BF)
             for m in range(8):
                 sends[m, 0:48, span] = d[m * 48 : (m + 1) * 48, :]
             if n == 0:
-                e = against(left_e[...], b_all, t)
+                e = against(left_e, b_turned, span)
                 head = e.astype(BF).astype(F32)
                 rest = e - head
                 for m in range(8):
@@ -462,6 +467,8 @@
             pltpu.VMEM((64, 2 * COLS), BF),
             pltpu.VMEM((2, ROWS, COLS), BF),
             pltpu.VMEM((2, ROWS, COLS), BF),
+            pltpu.VMEM((2 * COLS, ROWS), BF),
+            pltpu.VMEM((2 * COLS, ROWS), BF),
             pltpu.VMEM((8, 64, ROWS), BF),
             pltpu.VMEM((8, 48, ROWS), BF),
             pltpu.VMEM((8, 64, ROWS), BF),

time: 64.4 us -> 63.7 us (0.989)
  Pallas kernels: 63 us -> 61.6 us
    pallas_call x1, Pallas kernels: 63 us -> 61.6 us  [body(): pl.pallas_call(kernel, out_shape=jax.ShapeDtypeStruct((8, SEGP), F32), in...]
where the time goes in v4:
time: 63.7 us; the launch traced here: 62.9 us
  Pallas kernels  61.6 us (97%)
  local copies, waits for them, and re-layouts  1.31 us (2%)
    pallas_call x1, Pallas kernels, body(): pl.pallas_call(kernel, out_shape=jax.ShapeDtypeStruct((8, SEGP), F32), in...  61.6 us
    transpose x1, local copies, waits for them, and re-layouts, body(): return out[:, :SEG].T  1.31 us

profile of v4, /device:TPU:1, one launch (start us, length us, event | category | flops | bytes accessed | tf_op | source)
XLA Modules:
  0.0 62.9 jit_solution(5986523319676619927)
XLA Ops:
  0.0 61.6 %kernel_panel.1 = f32[8,384]{1,0:T(8,128)} custom-call(bf16[32,1000]{1,0:T(8,128)(2,1)} %v_hbm.1, bf16[32,1000]{1,0:T(8,128)(2,1)} %c_hbm.1, s32[1,128]{1,0:T(1,128)} %bitcast.4, s32[1,128]{1,0:T(1,128)} %bitcast.5, bf16[512,1024]{1,0:T(8,128)(2,1)} %w_ref.1, bf16[512,1024]{1,0:T(8,128)(2,1)} %b_ref.1), custom_call_target="tpu_custom_call" | custom-call | tf_op jit(solution)/shard_map/kernel_panel/pallas_call | solution.py:448
  61.6 1.3 %slice_bitcast_fusion = f32[375,8]{0,1:T(8,128)} fusion(f32[8,384]{1,0:T(8,128)} %kernel_panel.1), kind=kLoop, calls=%fused_computation | loop fusion | bytes 24000 | tf_op jit(solution)/shard_map/transpose | solution.py:500

commit v5 on v4

--- a/solution.py
+++ b/solution.py
@@ -13,7 +13,8 @@
 COLS = 1024
 NB = 1000
 NBP = 1024
-HALF = 6
+QUARTERS = ((2,), (1, 3), (0,))
+SENT = (32, 48, 32)
 SEG = 375
 SEGP = 384
 HUBS = (0, 3, -3, 6, -6)
@@ -36,7 +37,7 @@
     v_hbm, c_hbm, pv_hbm, pc_hbm, w_ref, b_ref, out_ref,
     v_ref, c_ref, pv_ref, pc_ref,
     hub, cpad, g_all, swap_out, swap_in, got, low_f32, turned, left, left_e,
-    w_all, b_all, w_turned, b_turned, send0, send1, recv0, recv1, panel, seg_out, seg_in, total, y_in,
+    w_all, b_all, w_turned, b_turned, send0, send1, send2, recv0, recv1, recv2, panel, seg_out, seg_in, total, y_in,
     loc_sem, wb_ssem, wb_rsem, a_ssem, a_rsem, s_ssem, s_rsem, g_ssem, g_rsem, h_ssem, h_rsem,
     f_ssem, f_rsem, b_ssem, b_rsem, c_ssem, c_rsem, y_ssem, y_rsem,
 ):
@@ -243,50 +244,49 @@
 
     left_e[...] = (turned[0:64, :] * turned[64:128, :]).astype(BF)
 
-    def against(lhs, rhs, span):
-        return jnp.dot(lhs[...], rhs[:, span], preferred_element_type=F32)
-
-    def band_of(parity, i):
-        return 3 * parity + i + 3 * (i // 3)
-
-    def plane_of(parity, i):
-        return 4 * parity + i + 4 * lax.div(i, 4)
-
-    near = lax.rem(lax.div(z, 4), 2)
-
-    def build(parity):
+    def place(n, i, size):
+        quarter = lax.rem(lax.div(z, 4) + QUARTERS[n][0] + 2 * lax.div(i, size), 4)
+        return quarter * size + lax.rem(i, size)
+
+    def build(n):
+        bands_here = 3 * len(QUARTERS[n])
+
         def step(m, _):
             tile = turned[pl.ds(pl.multiple_of(m * 8, 8), 8), :]
-            for p in range(HALF // 2):
-                pair = jnp.concatenate(
-                    [tile * low_f32[pl.ds(band_of(parity, 2 * p + k), 1), :] for k in range(2)], axis=0
-                )
-                left[pl.ds(pl.multiple_of(m * 48 + 16 * p, 16), 16), :] = pair.astype(BF)
+            for p in range(SENT[n] // 16):
+                pair = [
+                    tile * low_f32[pl.ds(place(n, i, 3), 1), :] if i < bands_here else jnp.zeros_like(tile)
+                    for i in (2 * p, 2 * p + 1)
+                ]
+                rows = pl.ds(pl.multiple_of(m * SENT[n] + 16 * p, 16), 16)
+                left[rows, :] = jnp.concatenate(pair, axis=0).astype(BF)
             return 0
 
         lax.fori_loop(0, 8, step, 0)
 
+    buffers = ((send0, recv0), (send1, recv1), (send2, recv2))
+
     def b_copy_to(n, m):
-        sends, recvs = ((send0, recv0), (send1, recv1))[n]
+        sends, recvs = buffers[n]
         return remote(sends.at[m], recvs.at[chip], b_ssem.at[n, m], b_rsem.at[n, chip], row, 8 * core + m)
 
-    order = (near, 1 - near)
-    for n in range(2):
-        sends, recvs = ((send0, recv0), (send1, recv1))[n]
-        build(order[n])
+    for n in range(3):
+        sends, recvs = buffers[n]
+        build(n)
 
         def mul(t, _, n=n, sends=sends):
             span = pl.ds(pl.multiple_of(t * 256, 256), 256)
-            d = against(left, w_turned, span).astype(BF)
-            for m in range(8):
-                sends[m, 0:48, span] = d[m * 48 : (m + 1) * 48, :]
+            size = SENT[n]
+            d = jnp.dot(left[0 : 8 * size, :], w_turned[:, span], preferred_element_type=F32)
             if n == 0:
-                e = against(left_e, b_turned, span)
-                head = e.astype(BF).astype(F32)
-                rest = e - head
+                e = jnp.dot(left_e[...], b_turned[:, span], preferred_element_type=F32)
                 for m in range(8):
-                    both = jnp.concatenate([head[m * 8 : m * 8 + 8], rest[m * 8 : m * 8 + 8]], axis=0)
-                    sends[m, 48:64, span] = both.astype(BF)
+                    both = jnp.concatenate([d[m * size : m * size + 24], e[m * 8 : m * 8 + 8]], axis=0)
+                    sends[m, :, span] = both.astype(BF)
+            else:
+                d = d.astype(BF)
+                for m in range(8):
+                    sends[m, :, span] = d[m * size : (m + 1) * size, :]
             return 0
 
         lax.fori_loop(0, 2, mul, 0)
@@ -325,7 +325,7 @@
     low_f32[:, 0:ROWS] = lax.dot_general(sel, points, NT, preferred_element_type=F32)
 
     def b_recv(n):
-        recvs = (recv0, recv1)[n]
+        recvs = buffers[n][1]
 
         def step(k, _):
             @pl.when(2 * k + lax.div(col, 8) != col)
@@ -340,21 +340,23 @@
         return remote(seg_out.at[i], seg_in.at[z], c_ssem.at[i], c_rsem.at[z], 2 * i + ylo, col)
 
     lane = iota((8, SEGP), 1)
-    for n in range(2):
-        recvs = (recv0, recv1)[n]
-        parity = order[n]
+    for n in range(3):
+        recvs = buffers[n][1]
+        count = 3 * len(QUARTERS[n])
         b_recv(n)
         d = recvs[0].astype(F32)
         for k in range(1, 8):
             d = d + recvs[k].astype(F32)
         if n == 0:
-            exch = 2.0 * (d[48:56] + d[56:64])
+            exch = 2.0 * d[24:32]
         comb = [
-            low_f32[pl.ds(band_of(parity, i), 1), 0:ROWS] * exch - vpt * d[i * 8 : i * 8 + 8] for i in range(HALF)
+            low_f32[pl.ds(place(n, i, 3), 1), 0:ROWS] * exch - vpt * d[i * 8 : i * 8 + 8] for i in range(count)
         ]
+        if count == 3:
+            comb.append(jnp.zeros_like(exch))
         comb = jnp.concatenate(comb, axis=0).astype(BF)
-        panel[...] = jnp.dot(comb, points, preferred_element_type=F32)
-        for zl in range(8):
+        panel[0 : SENT[n], :] = jnp.dot(comb, points, preferred_element_type=F32)
+        for zl in range(4 * len(QUARTERS[n])):
             halves = []
             for y in range(2):
                 start = SEG * (2 * zl + y)
@@ -367,10 +369,10 @@
                     more = pltpu.roll(panel[band0 * 8 + 8 : band0 * 8 + 16, :], NB - off, 1)[:, 0:SEGP]
                     seg = jnp.where(lane < NB - off, seg, more)
                 halves.append(seg)
-            seg_out[pl.ds(plane_of(parity, zl), 1)] = jnp.concatenate(halves, axis=0).astype(BF).reshape(1, 16, SEGP)
-
-        def c_start(i, _, parity=parity):
-            there = plane_of(parity, i)
+            seg_out[pl.ds(place(n, jnp.int32(zl), 4), 1)] = jnp.concatenate(halves, axis=0).astype(BF).reshape(1, 16, SEGP)
+
+        def c_start(i, _, n=n):
+            there = place(n, i, 4)
 
             @pl.when(there != z)
             def _():
@@ -382,7 +384,7 @@
 
             return 0
 
-        lax.fori_loop(0, 8, c_start, 0)
+        lax.fori_loop(0, 4 * len(QUARTERS[n]), c_start, 0)
 
     def c_recv(i, _):
         @pl.when(i != z)
@@ -428,8 +430,8 @@
 
         @pl.when(8 * core + i != col)
         def _():
-            b_copy_to(0, i).wait_send()
-            b_copy_to(1, i).wait_send()
+            for n in range(3):
+                b_copy_to(n, i).wait_send()
 
         return 0
 
@@ -463,16 +465,18 @@
             pltpu.VMEM((2, 2, 8, 80, 128), BF),
             pltpu.VMEM((16, 2 * COLS), F32),
             pltpu.VMEM((128, 2 * COLS), F32),
-            pltpu.VMEM((8 * HALF * 8, 2 * COLS), BF),
+            pltpu.VMEM((8 * 48, 2 * COLS), BF),
             pltpu.VMEM((64, 2 * COLS), BF),
             pltpu.VMEM((2, ROWS, COLS), BF),
             pltpu.VMEM((2, ROWS, COLS), BF),
             pltpu.VMEM((2 * COLS, ROWS), BF),
             pltpu.VMEM((2 * COLS, ROWS), BF),
-            pltpu.VMEM((8, 64, ROWS), BF),
+            pltpu.VMEM((8, 32, ROWS), BF),
             pltpu.VMEM((8, 48, ROWS), BF),
-            pltpu.VMEM((8, 64, ROWS), BF),
+            pltpu.VMEM((8, 32, ROWS), BF),
+            pltpu.VMEM((8, 32, ROWS), BF),
             pltpu.VMEM((8, 48, ROWS), BF),
+            pltpu.VMEM((8, 32, ROWS), BF),
             pltpu.VMEM((48, NBP), F32),
             pltpu.VMEM((NZ, 16, SEGP), BF),
             pltpu.VMEM((NZ, 16, SEGP), BF),
@@ -485,7 +489,7 @@
             dma((8,)), dma((8,)),
             dma((8,)), dma((8,)),
             dma, dma,
-            dma((2, 8)), dma((2, 8)),
+            dma((3, 8)), dma((3, 8)),
             dma((16,)), dma((16,)),
             dma, dma,
         ],

time: 63.7 us -> 61.8 us (0.970)
  Pallas kernels: 61.6 us -> 60.3 us
    pallas_call x1, Pallas kernels: 61.6 us -> 60.3 us  [body(): pl.pallas_call(kernel, out_shape=jax.ShapeDtypeStruct((8, SEGP), F32), in...]
where the time goes in v5:
time: 61.8 us; the launch traced here: 61.6 us
  Pallas kernels  60.3 us (98%)
  local copies, waits for them, and re-layouts  1.31 us (2%)
    pallas_call x1, Pallas kernels, body(): pl.pallas_call(kernel, out_shape=jax.ShapeDtypeStruct((8, SEGP), F32), in...  60.3 us
    transpose x1, local copies, waits for them, and re-layouts, body(): return out[:, :SEG].T  1.31 us

profile of v5, /device:TPU:1, one launch (start us, length us, event | category | flops | bytes accessed | tf_op | source)
XLA Modules:
  0.0 61.6 jit_solution(8505389374853698709)
XLA Ops:
  0.0 60.3 %kernel_panel.1 = f32[8,384]{1,0:T(8,128)} custom-call(bf16[32,1000]{1,0:T(8,128)(2,1)} %v_hbm.1, bf16[32,1000]{1,0:T(8,128)(2,1)} %c_hbm.1, s32[1,128]{1,0:T(1,128)} %bitcast.4, s32[1,128]{1,0:T(1,128)} %bitcast.5, bf16[512,1024]{1,0:T(8,128)(2,1)} %w_ref.1, bf16[512,1024]{1,0:T(8,128)(2,1)} %b_ref.1), custom_call_target="tpu_custom_call" | custom-call | tf_op jit(solution)/shard_map/kernel_panel/pallas_call | solution.py:450
  60.3 1.3 %slice_bitcast_fusion = f32[375,8]{0,1:T(8,128)} fusion(f32[8,384]{1,0:T(8,128)} %kernel_panel.1), kind=kLoop, calls=%fused_computation | loop fusion | bytes 24000 | tf_op jit(solution)/shard_map/transpose | solution.py:504

commit v6 on v5

--- a/solution.py
+++ b/solution.py
@@ -354,8 +354,12 @@
         ]
         if count == 3:
             comb.append(jnp.zeros_like(exch))
-        comb = jnp.concatenate(comb, axis=0).astype(BF)
-        panel[0 : SENT[n], :] = jnp.dot(comb, points, preferred_element_type=F32)
+        comb = jnp.concatenate(comb, axis=0)
+        head = comb.astype(BF)
+        rest = (comb - head.astype(F32)).astype(BF)
+        panel[0 : SENT[n], :] = jnp.dot(head, points, preferred_element_type=F32) + jnp.dot(
+            rest, points, preferred_element_type=F32
+        )
         for zl in range(4 * len(QUARTERS[n])):
             halves = []
             for y in range(2):

time: 61.8 us -> 62 us (level)
  no operation moved by 1% of the time
where the time goes in v6:
time: 62 us; the launch traced here: 61.8 us
  Pallas kernels  60.5 us (98%)
  local copies, waits for them, and re-layouts  1.31 us (2%)
    pallas_call x1, Pallas kernels, body(): pl.pallas_call(kernel, out_shape=jax.ShapeDtypeStruct((8, SEGP), F32), in...  60.5 us
    transpose x1, local copies, waits for them, and re-layouts, body(): return out[:, :SEG].T  1.31 us

profile of v6, /device:TPU:1, one launch (start us, length us, event | category | flops | bytes accessed | tf_op | source)
XLA Modules:
  0.0 61.8 jit_solution(4714717202699701207)
XLA Ops:
  0.0 60.5 %kernel_panel.1 = f32[8,384]{1,0:T(8,128)} custom-call(bf16[32,1000]{1,0:T(8,128)(2,1)} %v_hbm.1, bf16[32,1000]{1,0:T(8,128)(2,1)} %c_hbm.1, s32[1,128]{1,0:T(1,128)} %bitcast.4, s32[1,128]{1,0:T(1,128)} %bitcast.5, bf16[512,1024]{1,0:T(8,128)(2,1)} %w_ref.1, bf16[512,1024]{1,0:T(8,128)(2,1)} %b_ref.1), custom_call_target="tpu_custom_call" | custom-call | tf_op jit(solution)/shard_map/kernel_panel/pallas_call | solution.py:454
  60.5 1.3 %slice_bitcast_fusion = f32[375,8]{0,1:T(8,128)} fusion(f32[8,384]{1,0:T(8,128)} %kernel_panel.1), kind=kLoop, calls=%fused_computation | loop fusion | bytes 24000 | tf_op jit(solution)/shard_map/transpose | solution.py:508

commit v7 on v6

--- a/solution.py
+++ b/solution.py
@@ -201,6 +201,14 @@
         s_copy(n).wait_recv()
         a_start(n)
 
+    def h_start(i, _):
+        k = lax.rem(chip + i, 8)
+        remote(g_all.at[col], g_all.at[2 * k + core], g_ssem.at[k], g_rsem.at[k], row, mate).wait_recv()
+        h_copy(k, core).start()
+        return 0
+
+    lax.fori_loop(1, 8, h_start, 0)
+
     loads[4].wait()
     loads[5].wait()
     w_copy.wait_recv()
@@ -303,14 +311,6 @@
             return 0
 
         lax.fori_loop(0, 8, b_start, 0)
-
-    def h_start(i, _):
-        k = lax.rem(chip + i, 8)
-        remote(g_all.at[col], g_all.at[2 * k + core], g_ssem.at[k], g_rsem.at[k], row, mate).wait_recv()
-        h_copy(k, core).start()
-        return 0
-
-    lax.fori_loop(1, 8, h_start, 0)
 
     def h_wait(i, _):
         h_copy(i, 1 - core).wait_recv()

time: 62 us -> 61.1 us (0.985)
  Pallas kernels: 60.5 us -> 59.6 us
    pallas_call x1, Pallas kernels: 60.5 us -> 59.6 us  [body(): pl.pallas_call(kernel, out_shape=jax.ShapeDtypeStruct((8, SEGP), F32), in...]
where the time goes in v7:
time: 61.1 us; the launch traced here: 60.9 us
  Pallas kernels  59.6 us (98%)
  local copies, waits for them, and re-layouts  1.31 us (2%)
    pallas_call x1, Pallas kernels, body(): pl.pallas_call(kernel, out_shape=jax.ShapeDtypeStruct((8, SEGP), F32), in...  59.6 us
    transpose x1, local copies, waits for them, and re-layouts, body(): return out[:, :SEG].T  1.31 us

profile of v7, /device:TPU:1, one launch (start us, length us, event | category | flops | bytes accessed | tf_op | source)
XLA Modules:
  0.0 60.9 jit_solution(13285653302789085011)
XLA Ops:
  0.0 59.6 %kernel_panel.1 = f32[8,384]{1,0:T(8,128)} custom-call(bf16[32,1000]{1,0:T(8,128)(2,1)} %v_hbm.1, bf16[32,1000]{1,0:T(8,128)(2,1)} %c_hbm.1, s32[1,128]{1,0:T(1,128)} %bitcast.4, s32[1,128]{1,0:T(1,128)} %bitcast.5, bf16[512,1024]{1,0:T(8,128)(2,1)} %w_ref.1, bf16[512,1024]{1,0:T(8,128)(2,1)} %b_ref.1), custom_call_target="tpu_custom_call" | custom-call | tf_op jit(solution)/shard_map/kernel_panel/pallas_call | solution.py:454
  59.6 1.3 %slice_bitcast_fusion = f32[375,8]{0,1:T(8,128)} fusion(f32[8,384]{1,0:T(8,128)} %kernel_panel.1), kind=kLoop, calls=%fused_computation | loop fusion | bytes 24000 | tf_op jit(solution)/shard_map/transpose | solution.py:508

commit v8 on v7

--- a/solution.py
+++ b/solution.py
@@ -36,7 +36,7 @@
 def kernel(
     v_hbm, c_hbm, pv_hbm, pc_hbm, w_ref, b_ref, out_ref,
     v_ref, c_ref, pv_ref, pc_ref,
-    hub, cpad, g_all, swap_out, swap_in, got, low_f32, turned, left, left_e,
+    hub, cpad, g_all, row_low, row_vp, swap_out, swap_in, got, low_f32, turned, left, left_e,
     w_all, b_all, w_turned, b_turned, send0, send1, send2, recv0, recv1, recv2, panel, seg_out, seg_in, total, y_in,
     loc_sem, wb_ssem, wb_rsem, a_ssem, a_rsem, s_ssem, s_rsem, g_ssem, g_rsem, h_ssem, h_rsem,
     f_ssem, f_rsem, b_ssem, b_rsem, c_ssem, c_rsem, y_ssem, y_rsem,
@@ -224,6 +224,17 @@
 
     lax.fori_loop(0, 8, turn, 0)
 
+    def h_wait(i, _):
+        h_copy(i, 1 - core).wait_recv()
+        return 0
+
+    lax.fori_loop(0, 8, h_wait, 0)
+    mine = jnp.where(iota((8, 128), 1) == col * 8 + iota((8, 128), 0), pv_ref[...].astype(F32), 0.0)
+    sel = onehot(jnp.sum(mine, axis=1, keepdims=True) == iota((8, NBP), 1).astype(F32))
+    row_vp[...] = lax.dot_general(sel, g_all[...].reshape(ROWS, NBP), NT, preferred_element_type=F32)
+    sel = onehot((iota((16, NBP), 1) == iota((16, NBP), 0) + NB) & (iota((16, NBP), 0) < NCW))
+    row_low[...] = lax.dot_general(sel, g_all[...].reshape(ROWS, NBP), NT, preferred_element_type=F32)
+
     eye = onehot(iota((128, 128), 0) == iota((128, 128), 1))
 
     def arrive(e, y):
@@ -312,17 +323,7 @@
 
         lax.fori_loop(0, 8, b_start, 0)
 
-    def h_wait(i, _):
-        h_copy(i, 1 - core).wait_recv()
-        return 0
-
-    lax.fori_loop(0, 8, h_wait, 0)
     points = g_all[...].reshape(ROWS, NBP)
-    mine = jnp.where(iota((8, 128), 1) == col * 8 + iota((8, 128), 0), pv_ref[...].astype(F32), 0.0)
-    sel = onehot(jnp.sum(mine, axis=1, keepdims=True) == iota((8, NBP), 1).astype(F32))
-    vpt = lax.dot_general(sel, points, NT, preferred_element_type=F32)
-    sel = onehot((iota((16, NBP), 1) == iota((16, NBP), 0) + NB) & (iota((16, NBP), 0) < NCW))
-    low_f32[:, 0:ROWS] = lax.dot_general(sel, points, NT, preferred_element_type=F32)
 
     def b_recv(n):
         recvs = buffers[n][1]
@@ -350,7 +351,7 @@
         if n == 0:
             exch = 2.0 * d[24:32]
         comb = [
-            low_f32[pl.ds(place(n, i, 3), 1), 0:ROWS] * exch - vpt * d[i * 8 : i * 8 + 8] for i in range(count)
+            row_low[pl.ds(place(n, i, 3), 1), :] * exch - row_vp[...] * d[i * 8 : i * 8 + 8] for i in range(count)
         ]
         if count == 3:
             comb.append(jnp.zeros_like(exch))
@@ -464,6 +465,8 @@
             pltpu.VMEM((5, 80, 128), BF),
             pltpu.VMEM((128, NB), BF),
             pltpu.VMEM((NCOL, PTS, NBP), BF),
+            pltpu.VMEM((16, ROWS), F32),
+            pltpu.VMEM((8, ROWS), F32),
             pltpu.VMEM((48, 128), BF),
             pltpu.VMEM((48, 128), BF),
             pltpu.VMEM((2, 2, 8, 80, 128), BF),

time: 61.1 us -> 61.3 us (level)
  no operation moved by 1% of the time
where the time goes in v8:
time: 61.3 us; the launch traced here: 61.2 us
  Pallas kernels  59.8 us (98%)
  local copies, waits for them, and re-layouts  1.31 us (2%)
    pallas_call x1, Pallas kernels, body(): pl.pallas_call(kernel, out_shape=jax.ShapeDtypeStruct((8, SEGP), F32), in...  59.8 us
    transpose x1, local copies, waits for them, and re-layouts, body(): return out[:, :SEG].T  1.31 us

profile of v8, /device:TPU:1, one launch (start us, length us, event | category | flops | bytes accessed | tf_op | source)
XLA Modules:
  0.0 61.2 jit_solution(7976346596948128114)
XLA Ops:
  0.0 59.8 %kernel_panel.1 = f32[8,384]{1,0:T(8,128)} custom-call(bf16[32,1000]{1,0:T(8,128)(2,1)} %v_hbm.1, bf16[32,1000]{1,0:T(8,128)(2,1)} %c_hbm.1, s32[1,128]{1,0:T(1,128)} %bitcast.4, s32[1,128]{1,0:T(1,128)} %bitcast.5, bf16[512,1024]{1,0:T(8,128)(2,1)} %w_ref.1, bf16[512,1024]{1,0:T(8,128)(2,1)} %b_ref.1), custom_call_target="tpu_custom_call" | custom-call | tf_op jit(solution)/shard_map/kernel_panel/pallas_call | solution.py:455
  59.9 1.3 %slice_bitcast_fusion = f32[375,8]{0,1:T(8,128)} fusion(f32[8,384]{1,0:T(8,128)} %kernel_panel.1), kind=kLoop, calls=%fused_computation | loop fusion | bytes 24000 | tf_op jit(solution)/shard_map/transpose | solution.py:511
